TPU v7x, 32 devices: a whole 2x2x4 slice. The times are simulated.
32 devices in a mesh: ctx: 8 (over z, y), tp: 4 (over x, core).
Axes of the slice: x: 2, y: 2, z: 4, core: 2. Of those that a mesh axis runs over, the one named last changes fastest.
Arguments:
- tokens: float32 [4096, 1024], P(('ctx', 'tp')), may hold values from -6 to 6
- positions: int32 [4096], P('ctx'), may hold values from 0 to 4095, as said below
- q_weight: bfloat16 [1024, 2048], P('ctx', 'tp'), may hold values from -0.1875 to 0.1875
- k_weight: bfloat16 [1024, 1024], P('ctx', 'tp'), may hold values from -0.1875 to 0.1875
- v_weight: bfloat16 [1024, 1024], P('ctx', 'tp'), may hold values from -0.1875 to 0.1875
- o_weight: bfloat16 [2048, 1024], P('tp', 'ctx'), may hold values from -1.5 to 1.5
- gate_weight: bfloat16 [1024, 3072], P('ctx', 'tp'), may hold values from -0.1875 to 0.1875
- up_weight: bfloat16 [1024, 3072], P('ctx', 'tp'), may hold values from -0.1875 to 0.1875
- down_weight: bfloat16 [3072, 1024], P('tp', 'ctx'), may hold values from -0.109375 to 0.109375
- norm1_gain: float32 [1024], replicated, may hold values from 0.5 to 1.5
- norm2_gain: float32 [1024], replicated, may hold values from 0.5 to 1.5
- q_gain: float32 [128], replicated, may hold values from 0.5 to 1.6
- k_gain: float32 [128], replicated, may hold values from 0.5 to 1.6
- cotangent: float32 [4096, 1024], P(('ctx', 'tp')), may hold values from -6 to 6
Outputs:
- block_out: float32 [4096, 1024], P(('ctx', 'tp'))
- input_grad: float32 [4096, 1024], P(('ctx', 'tp'))
- q_weight_grad: float32 [1024, 2048], P('ctx', 'tp')
- k_weight_grad: float32 [1024, 1024], P('ctx', 'tp')
- v_weight_grad: float32 [1024, 1024], P('ctx', 'tp')
- o_weight_grad: float32 [2048, 1024], P('tp', 'ctx')
- gate_weight_grad: float32 [1024, 3072], P('ctx', 'tp')
- up_weight_grad: float32 [1024, 3072], P('ctx', 'tp')
- down_weight_grad: float32 [3072, 1024], P('tp', 'ctx')
- norm1_grad: float32 [1024], replicated
- norm2_grad: float32 [1024], replicated
- q_gain_grad: float32 [128], replicated
- k_gain_grad: float32 [128], replicated
Inputs may be any that keep to these rules, and one draw needn't show every extreme that they name: Each aligned block of 512 rows holds the positions b * 512 + i for i = 0 to 511 in order, for a block number b; every block number 0 to 7 occurs once.
All inputs are finite; a program needn't handle non-finite values.
Results may differ from a plain program's by a relative error of at most 0.022.
Values may be sent and summed in bfloat16 or wider, within the bound.
A program may use at most 192 MiB of HBM per device.

v0:
```python
import math

import jax
import jax.numpy as jnp
from jax import lax
from jax.sharding import PartitionSpec as P

DOCS = 2


EPSILON = 1e-06
ROPE_BASE = 1000000.0
MASKED = -1e30
KEY_SPAN = 512


def inv_rms(values):
    return lax.rsqrt(jnp.mean(values * values, axis=-1, keepdims=True) + EPSILON)


def rope_tables(positions, width):
    half_width = width // 2
    inverse = ROPE_BASE ** (-(jnp.arange(half_width, dtype=jnp.float32) * 2.0) / width)
    angles = positions.astype(jnp.float32)[:, None] * inverse[None, :]
    return (jnp.cos(angles), jnp.sin(angles))


def spread_table(table, values):
    half_width = values.shape[-1] // 2
    table_shape = (table.shape[0],) + (1,) * (values.ndim - 2) + (half_width,)
    return table.reshape(table_shape)


def rotate(values, cosine, sine_table):
    half_width = values.shape[-1] // 2
    cosine = spread_table(cosine, values)
    sine_table = spread_table(sine_table, values)
    former = values[..., :half_width]
    latter = values[..., half_width:]
    return jnp.concatenate(
        [former * cosine - latter * sine_table, latter * cosine + former * sine_table], axis=-1
    )


def rotate_back(grads, cosine, sine_table):
    half_width = grads.shape[-1] // 2
    cosine = spread_table(cosine, grads)
    sine_table = spread_table(sine_table, grads)
    former = grads[..., :half_width]
    latter = grads[..., half_width:]
    return jnp.concatenate(
        [former * cosine + latter * sine_table, latter * cosine - former * sine_table], axis=-1
    )


def norm_back(upstream, normed, inverse):
    return inverse * (upstream - normed * jnp.mean(upstream * normed, axis=-1, keepdims=True))


def contract_last(operand_left, operand_right):
    return lax.dot_general(
        operand_left, operand_right, (((1,), (1,)), ((), ())), preferred_element_type=jnp.float32
    )


def contract_rows(operand_left, operand_right):
    return lax.dot_general(
        operand_left, operand_right, (((0,), (0,)), ((), ())), preferred_element_type=jnp.float32
    )


def gather_rows(part_rows):
    return lax.all_gather(part_rows, "tp", axis=0, tiled=True)


def row_sums(products):
    summed = None
    for operand_left, operand_right, transposed in products:
        if transposed:
            product = contract_last(operand_left, operand_right)
        else:
            product = jnp.dot(operand_left, operand_right, preferred_element_type=jnp.float32)
        summed = product if summed is None else summed + product
    return lax.psum_scatter(
        summed.astype(jnp.bfloat16), "tp", scatter_dimension=0, tiled=True
    ).astype(jnp.float32)


def whole_keys(keys_local, values_local, positions):
    return (
        lax.all_gather(keys_local, "ctx", axis=0, tiled=True),
        lax.all_gather(values_local, "ctx", axis=0, tiled=True),
        lax.all_gather(positions, "ctx", axis=0, tiled=True),
    )


def step_length(length):
    return math.gcd(length, KEY_SPAN)


def allowed_mask(key_pos, query_pos, query_start):
    key_row = key_pos[None, None, None, :]
    return jnp.logical_and(
        key_row <= query_pos[None, None, :, None], key_row >= query_start[None, None, :, None]
    )


def outside(key_pos, query_pos, query_start):
    return jnp.logical_or(
        jnp.min(key_pos) > jnp.max(query_pos), jnp.max(key_pos) < jnp.min(query_start)
    )


def attend_block(
    carried, keys_part, values_part, key_pos, queries, query_pos, query_start, score_scale
):

    def attend_work(current):
        row_top, row_total, mixed_sum = current
        scores = (
            jnp.einsum("qgjd,kgd->gjqk", queries, keys_part, preferred_element_type=jnp.float32)
            * score_scale
        )
        allowed = allowed_mask(key_pos, query_pos, query_start)
        scores = jnp.where(allowed, scores, MASKED)
        new_top = jnp.maximum(row_top, jnp.max(scores, axis=-1))
        probs = jnp.where(allowed, jnp.exp(scores - new_top[..., None]), 0.0)
        factor = jnp.exp(row_top - new_top)
        row_total = row_total * factor + jnp.sum(probs, axis=-1)
        update = jnp.einsum(
            "gjqk,kgd->qgjd",
            probs.astype(jnp.bfloat16),
            values_part,
            preferred_element_type=jnp.float32,
        )
        mixed_sum = mixed_sum * jnp.transpose(factor, (2, 0, 1))[..., None] + update
        return (new_top, row_total, mixed_sum)

    return lax.cond(
        outside(key_pos, query_pos, query_start), lambda current: current, attend_work, carried
    )


def sweep_keys(
    carried, keys_part, values_part, key_pos, queries, query_pos, query_start, score_scale
):
    length = keys_part.shape[0]
    step_len = step_length(length)
    step_count = length // step_len

    def sweep_step(current, pieces):
        return (
            attend_block(
                current,
                pieces[0],
                pieces[1],
                pieces[2],
                queries,
                query_pos,
                query_start,
                score_scale,
            ),
            None,
        )

    stacked = (
        keys_part.reshape((step_count, step_len) + keys_part.shape[1:]),
        values_part.reshape((step_count, step_len) + values_part.shape[1:]),
        key_pos.reshape(step_count, step_len),
    )
    carried, unused = lax.scan(sweep_step, carried, stacked)
    return carried


def score_pair(keys_part, values_part, key_pos, query_side):
    queries, query_pos, query_start, grad_out, delta_rows, log_total, score_scale = query_side
    scores = (
        jnp.einsum("qgjd,kgd->gjqk", queries, keys_part, preferred_element_type=jnp.float32)
        * score_scale
    )
    allowed = allowed_mask(key_pos, query_pos, query_start)
    probs = jnp.where(allowed, jnp.exp(scores - log_total[..., None]), 0.0)
    prob_grad = jnp.einsum(
        "qgjd,kgd->gjqk", grad_out, values_part, preferred_element_type=jnp.float32
    )
    score_grad = probs * (prob_grad - delta_rows[..., None])
    return (probs.astype(jnp.bfloat16), score_grad.astype(jnp.bfloat16))


def stack_steps(all_keys, all_values, all_pos):
    length = all_keys.shape[0]
    step_len = step_length(length)
    step_count = length // step_len
    return (
        all_keys.reshape((step_count, step_len) + all_keys.shape[1:]),
        all_values.reshape((step_count, step_len) + all_values.shape[1:]),
        all_pos.reshape(step_count, step_len),
    )


def query_only(all_keys, all_values, all_pos, query_side):
    queries, query_pos, query_start, grad_out, delta_rows, log_total, score_scale = query_side

    def grad_step(current, pieces):
        keys_part, values_part, key_pos = pieces

        def grad_work(query_acc):
            probs_low, score_low = score_pair(keys_part, values_part, key_pos, query_side)
            return (
                query_acc
                + jnp.einsum(
                    "gjqk,kgd->qgjd", score_low, keys_part, preferred_element_type=jnp.float32
                )
                * score_scale
            )

        return (
            lax.cond(
                outside(key_pos, query_pos, query_start),
                lambda query_acc: query_acc,
                grad_work,
                current,
            ),
            None,
        )

    initial = jnp.zeros(queries.shape, jnp.float32)
    query_grad, unused = lax.scan(grad_step, initial, stack_steps(all_keys, all_values, all_pos))
    return query_grad


def key_rows(all_keys, all_values, all_pos, query_side, span_rows):
    queries, query_pos, query_start, grad_out, delta_rows, log_total, score_scale = query_side

    def term_step(unused, pieces):
        keys_part, values_part, key_pos = pieces

        def term_work(ignored):
            probs_low, score_low = score_pair(keys_part, values_part, key_pos, query_side)
            value_part = jnp.einsum(
                "gjqk,qgjd->kgd", probs_low, grad_out, preferred_element_type=jnp.float32
            )
            key_part = (
                jnp.einsum("gjqk,qgjd->kgd", score_low, queries, preferred_element_type=jnp.float32)
                * score_scale
            )
            return jnp.stack([key_part, value_part], axis=1)

        def skipped(ignored):
            return jnp.zeros((keys_part.shape[0], 2) + keys_part.shape[1:], jnp.float32)

        return (unused, lax.cond(outside(key_pos, query_pos, query_start), skipped, term_work, 0))

    unused, terms = lax.scan(term_step, 0, stack_steps(all_keys, all_values, all_pos))
    return terms.reshape((span_rows, 2) + all_keys.shape[1:])


def local(
    tokens,
    positions,
    q_weight,
    k_weight,
    v_weight,
    o_weight,
    gate_weight,
    up_weight,
    down_weight,
    norm1_gain,
    norm2_gain,
    q_gain,
    k_gain,
    cotangent,
):
    head_width = q_gain.shape[0]
    score_scale = head_width ** (-0.5)
    local_heads = q_weight.shape[1] // head_width
    local_groups = k_weight.shape[1] // head_width
    group_size = local_heads // local_groups
    doc_len = positions.shape[0] * lax.axis_size("ctx") // DOCS
    wq_full, wk_full, wv_full, wg_full, wu_full, wo_full, wd_full = (
        lax.all_gather(q_weight, "ctx", axis=0, tiled=True),
        lax.all_gather(k_weight, "ctx", axis=0, tiled=True),
        lax.all_gather(v_weight, "ctx", axis=0, tiled=True),
        lax.all_gather(gate_weight, "ctx", axis=0, tiled=True),
        lax.all_gather(up_weight, "ctx", axis=0, tiled=True),
        lax.all_gather(o_weight, "ctx", axis=1, tiled=True),
        lax.all_gather(down_weight, "ctx", axis=1, tiled=True),
    )
    inv_first = inv_rms(tokens)
    normed_first = tokens * inv_first
    hidden_first = gather_rows((normed_first * norm1_gain).astype(jnp.bfloat16))
    block_len = hidden_first.shape[0]
    local_pos = positions % doc_len
    query_start = positions - local_pos
    cosine, sine_table = rope_tables(local_pos, head_width)
    query_raw = jnp.dot(hidden_first, wq_full, preferred_element_type=jnp.float32).reshape(
        block_len, local_groups, group_size, head_width
    )
    key_raw = jnp.dot(hidden_first, wk_full, preferred_element_type=jnp.float32).reshape(
        block_len, local_groups, head_width
    )
    values_local = (
        jnp.dot(hidden_first, wv_full, preferred_element_type=jnp.float32)
        .astype(jnp.bfloat16)
        .reshape(block_len, local_groups, head_width)
    )
    inv_query = inv_rms(query_raw)
    query_hat = query_raw * inv_query
    queries = rotate(query_hat * q_gain, cosine, sine_table).astype(jnp.bfloat16)
    inv_key = inv_rms(key_raw)
    key_hat = key_raw * inv_key
    keys_local = rotate(key_hat * k_gain, cosine, sine_table).astype(jnp.bfloat16)
    initial = (
        jnp.full((local_groups, group_size, block_len), MASKED, jnp.float32),
        jnp.zeros((local_groups, group_size, block_len), jnp.float32),
        jnp.zeros((block_len, local_groups, group_size, head_width), jnp.float32),
    )
    row_top, row_total, mixed_sum = sweep_keys(
        initial,
        lax.all_gather(keys_local, "ctx", axis=0, tiled=True),
        lax.all_gather(values_local, "ctx", axis=0, tiled=True),
        lax.all_gather(positions, "ctx", axis=0, tiled=True),
        queries,
        positions,
        query_start,
        score_scale,
    )
    attended = (mixed_sum / jnp.transpose(row_total, (2, 0, 1))[..., None]).astype(jnp.bfloat16)
    log_total = row_top + jnp.log(row_total)
    attended_flat = attended.reshape(block_len, local_heads * head_width)
    middle = tokens + row_sums([(attended_flat, wo_full, False)])
    inv_second = inv_rms(middle)
    normed_second = middle * inv_second
    hidden_second = gather_rows((normed_second * norm2_gain).astype(jnp.bfloat16))
    gate = jnp.dot(hidden_second, wg_full, preferred_element_type=jnp.float32)
    up_proj = jnp.dot(hidden_second, wu_full, preferred_element_type=jnp.float32)
    sigmoid = jax.nn.sigmoid(gate)
    activation = (gate * sigmoid * up_proj).astype(jnp.bfloat16)
    block_out = middle + row_sums([(activation, wd_full, False)])
    cot_low = gather_rows(cotangent.astype(jnp.bfloat16))
    act_grad = contract_last(cot_low, wd_full)
    down_grad = contract_rows(activation, cot_low)
    gate_grad = (act_grad * up_proj * sigmoid * (1.0 + gate * (1.0 - sigmoid))).astype(jnp.bfloat16)
    up_grad = (act_grad * gate * sigmoid).astype(jnp.bfloat16)
    hidden2_grad = row_sums([(gate_grad, wg_full, True), (up_grad, wu_full, True)])
    gate_wgrad = contract_rows(hidden_second, gate_grad)
    up_wgrad = contract_rows(hidden_second, up_grad)
    norm2_part = jnp.sum(hidden2_grad * normed_second, axis=0)
    middle_grad = norm_back(hidden2_grad * norm2_gain, normed_second, inv_second) + cotangent
    mid_low = gather_rows(middle_grad.astype(jnp.bfloat16))
    attended_grad = contract_last(mid_low, wo_full).astype(jnp.bfloat16)
    out_wgrad = contract_rows(attended_flat, mid_low)
    grad_out = attended_grad.reshape(block_len, local_groups, group_size, head_width)
    delta_rows = jnp.transpose(
        jnp.sum(grad_out.astype(jnp.float32) * attended.astype(jnp.float32), axis=-1), (1, 2, 0)
    )
    all_keys, all_values, all_pos = whole_keys(keys_local, values_local, positions)
    query_side = (queries, positions, query_start, grad_out, delta_rows, log_total, score_scale)
    query_grad = query_only(all_keys, all_values, all_pos, query_side)
    stacked_grads = lax.psum_scatter(
        key_rows(
            all_keys, all_values, all_pos, query_side, block_len * lax.axis_size("ctx")
        ).astype(jnp.bfloat16),
        "ctx",
        scatter_dimension=0,
        tiled=True,
    ).astype(jnp.float32)
    key_grad = stacked_grads[:, 0]
    value_grad = stacked_grads[:, 1]
    query_back = rotate_back(query_grad, cosine, sine_table)
    q_gain_part = jnp.sum(query_back * query_hat, axis=(0, 1, 2))
    query_raw_grad = (
        norm_back(query_back * q_gain, query_hat, inv_query)
        .astype(jnp.bfloat16)
        .reshape(block_len, local_heads * head_width)
    )
    key_back = rotate_back(key_grad, cosine, sine_table)
    k_gain_part = jnp.sum(key_back * key_hat, axis=(0, 1))
    key_raw_grad = (
        norm_back(key_back * k_gain, key_hat, inv_key)
        .astype(jnp.bfloat16)
        .reshape(block_len, local_groups * head_width)
    )
    value_low = value_grad.astype(jnp.bfloat16).reshape(block_len, local_groups * head_width)
    hidden1_grad = row_sums(
        [(query_raw_grad, wq_full, True), (key_raw_grad, wk_full, True), (value_low, wv_full, True)]
    )
    query_wgrad = contract_rows(hidden_first, query_raw_grad)
    key_wgrad = contract_rows(hidden_first, key_raw_grad)
    value_wgrad = contract_rows(hidden_first, value_low)
    norm1_part = jnp.sum(hidden1_grad * normed_first, axis=0)
    input_grad = norm_back(hidden1_grad * norm1_gain, normed_first, inv_first) + middle_grad
    q_wgrad, k_wgrad, v_wgrad, g_wgrad, u_wgrad, o_wgrad, d_wgrad = (
        lax.psum_scatter(
            query_wgrad.astype(jnp.bfloat16), "ctx", scatter_dimension=0, tiled=True
        ).astype(jnp.float32),
        lax.psum_scatter(
            key_wgrad.astype(jnp.bfloat16), "ctx", scatter_dimension=0, tiled=True
        ).astype(jnp.float32),
        lax.psum_scatter(
            value_wgrad.astype(jnp.bfloat16), "ctx", scatter_dimension=0, tiled=True
        ).astype(jnp.float32),
        lax.psum_scatter(
            gate_wgrad.astype(jnp.bfloat16), "ctx", scatter_dimension=0, tiled=True
        ).astype(jnp.float32),
        lax.psum_scatter(
            up_wgrad.astype(jnp.bfloat16), "ctx", scatter_dimension=0, tiled=True
        ).astype(jnp.float32),
        lax.psum_scatter(
            out_wgrad.astype(jnp.bfloat16), "ctx", scatter_dimension=1, tiled=True
        ).astype(jnp.float32),
        lax.psum_scatter(
            down_grad.astype(jnp.bfloat16), "ctx", scatter_dimension=1, tiled=True
        ).astype(jnp.float32),
    )
    norm1_grad, norm2_grad, q_gain_grad, k_gain_grad = lax.psum(
        (norm1_part, norm2_part, q_gain_part, k_gain_part), ("ctx", "tp")
    )
    return (
        block_out,
        input_grad,
        q_wgrad,
        k_wgrad,
        v_wgrad,
        o_wgrad,
        g_wgrad,
        u_wgrad,
        d_wgrad,
        norm1_grad,
        norm2_grad,
        q_gain_grad,
        k_gain_grad,
    )


def solution(mesh):
    in_specs = (
        P(("ctx", "tp"), None),
        P("ctx"),
        P("ctx", "tp"),
        P("ctx", "tp"),
        P("ctx", "tp"),
        P("tp", "ctx"),
        P("ctx", "tp"),
        P("ctx", "tp"),
        P("tp", "ctx"),
        P(),
        P(),
        P(),
        P(),
        P(("ctx", "tp"), None),
    )
    out_specs = (
        P(("ctx", "tp"), None),
        P(("ctx", "tp"), None),
        P("ctx", "tp"),
        P("ctx", "tp"),
        P("ctx", "tp"),
        P("tp", "ctx"),
        P("ctx", "tp"),
        P("ctx", "tp"),
        P("tp", "ctx"),
        P(),
        P(),
        P(),
        P(),
    )
    return jax.shard_map(local, mesh=mesh, in_specs=in_specs, out_specs=out_specs, check_vma=False)
```

profile of v0, /device:TPU:9, one launch (start us, length us, event | category | flops | bytes accessed | tf_op | source)
XLA Modules:
  0.0 1199.9 jit_solution(1241371477727722178)
XLA Ops:
  11.1 23.5 %all_gather.50 = bf16[1024,256]{1,0:T(8,128)(2,1)S(1)} all-gather(bf16[128,256]{1,0:T(8,128)(2,1)} %param.30), channel_id=1, replica_groups=mesh['ctx'=8,'tp'=4] {'ctx'}, dimensions={0}, use_global_device_ids=true | all-gather | bytes 589824 | tf_op jit(solution)/shard_map/all_gather | solution.py:283
  38.2 27.3 %all_gather.47 = bf16[1024,256]{1,0:T(8,128)(2,1)S(1)} all-gather(bf16[128,256]{1,0:T(8,128)(2,1)S(1)} %copy-done.26), channel_id=1, replica_groups=mesh['ctx'=8,'tp'=4] {'ctx'}, dimensions={0}, use_global_device_ids=true | all-gather | bytes 589824 | tf_op jit(solution)/shard_map/all_gather | solution.py:282
  69.3 22.3 %all-gather = s32[8,1,512]{2,1,0:T(1,128)S(1)} all-gather(s32[1,1,512]{2,1,0:T(1,128)S(1)} %bitcast.295), channel_id=1, replica_groups=mesh['ctx'=8,'tp'=4] {'ctx'}, dimensions={0}, use_global_device_ids=true | all-gather | bytes 18432 | tf_op jit(solution)/shard_map/all_gather | solution.py:322
  97.5 26.2 %all-gather.19.cloned.1.call-done = bf16[4096,2,128]{2,0,1:T(8,128)(2,1)} async-done(((bf16[512,2,128]{2,0,1:T(8,128)(2,1)}), bf16[4096,2,128]{2,0,1:T(8,128)(2,1)}) %all-gather.19.cloned.1.call-update) | async-done | bytes 2097168 | tf_op jit(solution)/shard_map/all_gather | solution.py:321
  126.9 47.2 %all-gather.15.cloned.1.call-done = bf16[4096,2,128]{2,0,1:T(8,128)(2,1)} async-done(((bf16[512,2,128]{2,0,1:T(8,128)(2,1)}), bf16[4096,2,128]{2,0,1:T(8,128)(2,1)}) %all-gather.15.cloned.1.call-update) | async-done | bytes 2097168 | tf_op jit(solution)/shard_map/all_gather | solution.py:320
  178.3 44.6 %while.40 = (s32[]{:T(128)}, f32[2,2,512]{2,1,0:T(2,128)S(1)}, f32[2,2,512]{2,1,0:T(2,128)S(1)}, f32[512,2,2,128]{3,0,2,1:T(8,128)}, s32[8,512]{1,0:T(8,128)S(1)...) while((s32[]{:T(128)}, f32[2,2,512]{2,1,0:T(2,128)S(1)}, ...), condition=%wide.region_12.13_spmd, body=%wide.region_5.12_spmd.sunk | while | flops 551820288 | bytes 25308516 | solution.py:171
  231.6 28.4 %reduce-scatter.17.cloned.1.call-done = bf16[128,1024]{1,0:T(8,128)(2,1)} async-done(((bf16[512,1024]{1,0:T(8,128)(2,1)}), bf16[128,1024]{1,0:T(8,128)(2,1)}) %reduce-scatter.17.cloned.1.call-update) | async-done | bytes 262160 | tf_op jit(solution)/shard_map/reduce_scatter | solution.py:84
  265.4 41.0 %all-gather.27.cloned.1.call-done = bf16[1024,768]{1,0:T(8,128)(2,1)} async-done(((bf16[128,768]{1,0:T(8,128)(2,1)}), bf16[1024,768]{1,0:T(8,128)(2,1)}) %all-gather.27.cloned.1.call-update) | async-done | bytes 1572880 | tf_op jit(solution)/shard_map/all_gather | solution.py:285
  306.3 18.4 %all-gather.23.cloned.1.call-done = bf16[512,1024]{1,0:T(8,128)(2,1)} async-done(((bf16[128,1024]{1,0:T(8,128)(2,1)}), bf16[512,1024]{1,0:T(8,128)(2,1)}) %all-gather.23.cloned.1.call-update) | async-done | bytes 1048592 | tf_op jit(solution)/shard_map/all_gather | solution.py:73
  328.6 42.1 %all-gather.25.cloned.1.call-done = bf16[1024,768]{1,0:T(8,128)(2,1)} async-done(((bf16[128,768]{1,0:T(8,128)(2,1)}), bf16[1024,768]{1,0:T(8,128)(2,1)}) %all-gather.25.cloned.1.call-update) | async-done | bytes 1572880 | tf_op jit(solution)/shard_map/all_gather | solution.py:284
  389.0 44.7 %all-gather.29.cloned.1.call-done = bf16[768,1024]{1,0:T(8,128)(2,1)} async-done(((bf16[768,128]{1,0:T(8,128)(2,1)}), bf16[768,1024]{1,0:T(8,128)(2,1)}) %all-gather.29.cloned.1.call-update) | async-done | bytes 1572880 | tf_op jit(solution)/shard_map/all_gather | solution.py:287
  443.0 25.7 %reduce-scatter.21.cloned.1.call-done = bf16[128,1024]{1,0:T(8,128)(2,1)} async-done(((bf16[512,1024]{1,0:T(8,128)(2,1)}), bf16[128,1024]{1,0:T(8,128)(2,1)}) %reduce-scatter.21.cloned.1.call-update) | async-done | bytes 262160 | tf_op jit(solution)/shard_map/reduce_scatter | solution.py:84
  472.0 17.2 %all-gather.33.cloned.1.call-done = bf16[512,1024]{1,0:T(8,128)(2,1)} async-done(((bf16[128,1024]{1,0:T(8,128)(2,1)}), bf16[512,1024]{1,0:T(8,128)(2,1)}) %all-gather.33.cloned.1.call-update) | async-done | bytes 1048592 | tf_op jit(solution)/shard_map/all_gather | solution.py:73
  492.6 70.1 %while.42 = (s32[]{:T(128)}, bf16[8,512,2,2,128]{4,1,0,3,2:T(8,128)(2,1)}, s32[8,512]{1,0:T(8,128)S(1)}, s32[]{:T(128)}, s32[]{:T(128)}, /*index=5*/s32[512]{0:T...) while((s32[]{:T(128)}, ...), condition=%wide.region_31.32_spmd, body=%wide.region_26.0_spmd.sunk | while | flops 1085539328 | bytes 19697448 | solution.py:254
  583.2 55.4 %while.41 = (s32[]{:T(128)}, f32[512,2,2,128]{3,0,2,1:T(8,128)}, s32[8,512]{1,0:T(8,128)S(1)}, s32[]{:T(128)}, s32[]{:T(128)}, /*index=5*/s32[512]{0:T(512)S(1)}...) while((s32[]{:T(128)}, f32[512,2,2,128]{3,0,2,1:T(8,128)}, ...), condition=%wide.region_24.25_spmd, body=%wide.region_19.24_spmd.sunk | while | flops 812909568 | bytes 12873491 | solution.py:228
  679.0 47.3 %reduce-scatter.39.cloned.1.call-done = bf16[128,768]{1,0:T(8,128)(2,1)} async-done(((bf16[1024,768]{1,0:T(8,128)(2,1)}), bf16[128,768]{1,0:T(8,128)(2,1)}) %reduce-scatter.39.cloned.1.call-update) | async-done | bytes 196624
  728.2 65.1 %reduce-scatter.35.cloned.1.call-done = bf16[128,768]{1,0:T(8,128)(2,1)} async-done(((bf16[1024,768]{1,0:T(8,128)(2,1)}), bf16[128,768]{1,0:T(8,128)(2,1)}) %reduce-scatter.35.cloned.1.call-update) | async-done | bytes 196624 | tf_op jit(solution)/shard_map/reduce_scatter | solution.py:406
  795.0 66.0 %reduce-scatter.33.cloned.1.call-done = bf16[128,768]{1,0:T(8,128)(2,1)} async-done(((bf16[1024,768]{1,0:T(8,128)(2,1)}), bf16[128,768]{1,0:T(8,128)(2,1)}) %reduce-scatter.33.cloned.1.call-update) | async-done | bytes 196624 | tf_op jit(solution)/shard_map/reduce_scatter | solution.py:403
  862.8 63.3 %reduce-scatter.37.cloned.1.call-done = bf16[128,512]{1,0:T(8,128)(2,1)} async-done(((bf16[1024,512]{1,0:T(8,128)(2,1)}), bf16[128,512]{1,0:T(8,128)(2,1)}) %reduce-scatter.37.cloned.1.call-update) | async-done | bytes 131088
  927.9 64.4 %reduce-scatter.27.cloned.1.call-done = bf16[128,512]{1,0:T(8,128)(2,1)} async-done(((bf16[1024,512]{1,0:T(8,128)(2,1)}), bf16[128,512]{1,0:T(8,128)(2,1)}) %reduce-scatter.27.cloned.1.call-update) | async-done | bytes 131088 | tf_op jit(solution)/shard_map/reduce_scatter | solution.py:394
  994.0 62.6 %reduce-scatter.31.cloned.1.call-done = bf16[128,256]{1,0:T(8,128)(2,1)} async-done(((bf16[1024,256]{1,0:T(8,128)(2,1)}), bf16[128,256]{1,0:T(8,128)(2,1)}) %reduce-scatter.31.cloned.1.call-update) | async-done | bytes 65552 | tf_op jit(solution)/shard_map/reduce_scatter | solution.py:400
  1058.1 63.7 %reduce-scatter.29.cloned.1.call-done = bf16[128,256]{1,0:T(8,128)(2,1)} async-done(((bf16[1024,256]{1,0:T(8,128)(2,1)}), bf16[128,256]{1,0:T(8,128)(2,1)}) %reduce-scatter.29.cloned.1.call-update) | async-done | bytes 65552 | tf_op jit(solution)/shard_map/reduce_scatter | solution.py:397
  1123.4 27.0 %reduce-scatter.25.cloned.1.call-done = bf16[128,1024]{1,0:T(8,128)(2,1)} async-done(((bf16[512,1024]{1,0:T(8,128)(2,1)}), bf16[128,1024]{1,0:T(8,128)(2,1)}) %reduce-scatter.25.cloned.1.call-update) | async-done | bytes 262160 | tf_op jit(solution)/shard_map/reduce_scatter | solution.py:84
  1151.6 39.1 %all-reduce = (f32[1024]{0:T(1024)}, f32[1024]{0:T(1024)}, f32[128]{0:T(128)}, f32[128]{0:T(128)}) all-reduce(f32[1024]{0:T(1024)S(1)} %get-tuple-element.849, f32[1024]{0:T(1024)S(1)} %get-tuple-element.847, f32[128]{0:T(128)S(1)} %reduce_sum.155, f32[128]{0:T(128)S(1)} %bitcast_reduce_fusion), channel_id=1, replica_groups=mesh['ctx'=8,'tp'=4] {'ctx','tp'}, use_global_device_ids=true, to_apply=%region_44.45 | all-reduce | flops 2304 | bytes 18432 | tf_op jit(solution)/shard_map/psum | solution.py:416
  (337 shorter events, 343.5 us)
Async XLA Ops:
  7.2 27.5 %all-gather.13.cloned.1.call-start = ((), (), s32[]{:S(2)}) async-start(), calls=%async_computation.12 | async-start | bytes 1310720 | tf_op jit(solution)/shard_map/all_gather | solution.py:73
  10.3 81.3 %all-gather.17.cloned.1.call-start = ((), (), s32[]{:S(2)}) async-start(), calls=%async_computation.14 | async-start | bytes 1179648 | tf_op jit(solution)/shard_map/all_gather | solution.py:281
  11.1 112.6 %all-gather.19.cloned.1.call-start = ((), (), s32[]{:S(2)}) async-start(), calls=%async_computation.15 | async-start | bytes 2359296 | tf_op jit(solution)/shard_map/all_gather | solution.py:321
  37.5 136.6 %all-gather.15.cloned.1.call-start = ((), (), s32[]{:S(2)}) async-start(), calls=%async_computation.13 | async-start | bytes 2359296 | tf_op jit(solution)/shard_map/all_gather | solution.py:320
  68.7 158.2 %all-gather.21.cloned.1.call-start = ((), (), s32[]{:S(2)}) async-start(), calls=%async_computation.16 | async-start | bytes 1179648 | tf_op jit(solution)/shard_map/all_gather | solution.py:286
  69.3 190.7 %reduce-scatter.17.cloned.1.call-start = ((), (), s32[]{:S(2)}) async-start(), calls=%async_computation.17 | async-start | bytes 1310720 | tf_op jit(solution)/shard_map/reduce_scatter | solution.py:84
  230.8 75.5 %all-gather.27.cloned.1.call-start = ((), (), s32[]{:S(2)}) async-start(), calls=%async_computation.20 | async-start | bytes 1769472 | tf_op jit(solution)/shard_map/all_gather | solution.py:285
  231.5 93.2 %all-gather.23.cloned.1.call-start = ((), (), s32[]{:S(2)}) async-start(), calls=%async_computation.18 | async-start | bytes 1310720 | tf_op jit(solution)/shard_map/all_gather | solution.py:73
  262.8 107.9 %all-gather.25.cloned.1.call-start = ((), (), s32[]{:S(2)}) async-start(), calls=%async_computation.19 | async-start | bytes 1769472 | tf_op jit(solution)/shard_map/all_gather | solution.py:284
  263.6 125.4 %all-gather.31.cloned.1.call-start = ((), (), s32[]{:S(2)}) async-start(), calls=%async_computation.23 | async-start | bytes 1310720 | tf_op jit(solution)/shard_map/all_gather | solution.py:73
  264.6 169.1 %all-gather.29.cloned.1.call-start = ((), (), s32[]{:S(2)}) async-start(), calls=%async_computation.21 | async-start | bytes 1769472 | tf_op jit(solution)/shard_map/all_gather | solution.py:287
  265.3 203.4 %reduce-scatter.21.cloned.1.call-start = ((), (), s32[]{:S(2)}) async-start(), calls=%async_computation.24 | async-start | bytes 1310720 | tf_op jit(solution)/shard_map/reduce_scatter | solution.py:84
  443.0 46.2 %all-gather.33.cloned.1.call-start = ((), (), s32[]{:S(2)}) async-start(), calls=%async_computation.25 | async-start | bytes 1310720 | tf_op jit(solution)/shard_map/all_gather | solution.py:73
  471.9 188.3 %reduce-scatter.23.cloned.1.call-start = ((), (), s32[]{:S(2)}) async-start(), calls=%async_computation.26 | async-start | bytes 4718592 | tf_op jit(solution)/shard_map/reduce_scatter | solution.py:360
  562.8 163.6 %reduce-scatter.39.cloned.1.call-start = ((), (), s32[]{:S(2)}) async-start(), calls=%async_computation.34 | async-start | bytes 1769472
  569.1 224.3 %reduce-scatter.35.cloned.1.call-start = ((), (), s32[]{:S(2)}) async-start(), calls=%async_computation.32 | async-start | bytes 1769472 | tf_op jit(solution)/shard_map/reduce_scatter | solution.py:406
  573.0 288.1 %reduce-scatter.33.cloned.1.call-start = ((), (), s32[]{:S(2)}) async-start(), calls=%async_computation.31 | async-start | bytes 1769472 | tf_op jit(solution)/shard_map/reduce_scatter | solution.py:403
  576.8 349.4 %reduce-scatter.37.cloned.1.call-start = ((), (), s32[]{:S(2)}) async-start(), calls=%async_computation.33 | async-start | bytes 1179648
  582.1 410.2 %reduce-scatter.27.cloned.1.call-start = ((), (), s32[]{:S(2)}) async-start(), calls=%async_computation.28 | async-start | bytes 1179648 | tf_op jit(solution)/shard_map/reduce_scatter | solution.py:394
  648.4 408.2 %reduce-scatter.31.cloned.1.call-start = ((), (), s32[]{:S(2)}) async-start(), calls=%async_computation.30 | async-start | bytes 589824 | tf_op jit(solution)/shard_map/reduce_scatter | solution.py:400
  666.1 455.8 %reduce-scatter.29.cloned.1.call-start = ((), (), s32[]{:S(2)}) async-start(), calls=%async_computation.29 | async-start | bytes 589824 | tf_op jit(solution)/shard_map/reduce_scatter | solution.py:397
  670.6 479.8 %reduce-scatter.25.cloned.1.call-start = ((), (), s32[]{:S(2)}) async-start(), calls=%async_computation.27 | async-start | bytes 1310720 | tf_op jit(solution)/shard_map/reduce_scatter | solution.py:84
  675.5 515.1 %reduce-scatter.19.cloned.1.call-start = ((), (), s32[]{:S(2)}) async-start(), calls=%async_computation.22 | async-start | bytes 1310720 | tf_op jit(solution)/shard_map/reduce_scatter | solution.py:84
  679.0 471.3 %copy-start.27 = (f32[1024]{0:T(1024)S(1)}, f32[1024]{0:T(1024)}, u32[]{:S(2)}) copy-start(f32[1024]{0:T(1024)} %param.35) | copy-start | bytes 12292
  (40 other events, 1277.9 us)
Sparse Core Ops, SparseCore 0:
  10.5 18.2 all-gather.12
  30.9 41.5 all-gather.16
  75.2 48.4 all-gather.18
  126.3 47.7 all-gather.14
  176.0 36.4 all-gather.20
  230.9 28.9 reduce-scatter.16
  262.3 43.9 all-gather.26
  308.5 16.1 all-gather.22
  327.2 43.5 all-gather.24
  372.8 16.1 all-gather.30
  391.3 42.3 all-gather.28
  443.1 25.5 reduce-scatter.20
  472.0 17.1 all-gather.32
  562.9 97.2 reduce-scatter.22
  663.8 62.4 reduce-scatter.38
  729.6 63.6 reduce-scatter.34
  797.0 64.0 reduce-scatter.32
  864.3 61.7 reduce-scatter.36
  929.9 62.3 reduce-scatter.26
  995.5 61.0 reduce-scatter.30
  1060.9 60.8 reduce-scatter.28
  1124.4 25.9 reduce-scatter.24
  1153.0 24.8 reduce-scatter.18
where the time goes:
time: 1210 us; the launch traced here: 1200 us
  waiting for transfers between devices  780 us (64%)
  matrix products  131 us (11%)
  blocking collectives  112 us (9%)
  loops' own time  63.5 us (5%)
  other arithmetic  58.9 us (5%)
  local copies, waits for them, and re-layouts  37.4 us (3%)
  between operations  15 us (1%)
    unnamed x25, waiting for transfers between devices  114 us
    reduce_scatter x4, waiting for transfers between devices, row_sums(): lax.psum_scatter(summed.astype(jnp.bfloat16), 'tp', scatter_dimension=0,...  81 us
    reduce_scatter x1, waiting for transfers between devices, local(): lax.psum_scatter(gate_wgrad.astype(jnp.bfloat16), 'ctx', scatter_dimensio...  66 us
    reduce_scatter x1, waiting for transfers between devices, local(): lax.psum_scatter(up_wgrad.astype(jnp.bfloat16), 'ctx', scatter_dimension=...  65.1 us
    reduce_scatter x1, waiting for transfers between devices, local(): lax.psum_scatter(query_wgrad.astype(jnp.bfloat16), 'ctx', scatter_dimensi...  64.4 us
    reduce_scatter x1, waiting for transfers between devices, local(): lax.psum_scatter(key_wgrad.astype(jnp.bfloat16), 'ctx', scatter_dimension...  63.7 us
    reduce_scatter x1, waiting for transfers between devices, local(): lax.psum_scatter(value_wgrad.astype(jnp.bfloat16), 'ctx', scatter_dimensi...  62.6 us
    all_gather x4, waiting for transfers between devices, gather_rows(): return lax.all_gather(part_rows, 'tp', axis=0, tiled=True)  50 us
  transfers between devices with their start and end apart: 23, of which 19 were waited for; matrix products, arithmetic and copies ran while one was open for 13% of the time, Pallas kernels for 0%

commit v1 on v0

v1 whole, which is shorter than its diff:
```python
import functools
import math

import jax
import jax.numpy as jnp
from jax import lax
from jax.experimental import pallas as pl
from jax.experimental.pallas import tpu as pltpu
from jax.sharding import PartitionSpec as P

DOCS = 2


EPSILON = 1e-06
ROPE_BASE = 1000000.0
MASKED = -1e30
KEY_SPAN = 512
MESH = pl.DeviceIdType.MESH


def inv_rms(values):
    return lax.rsqrt(jnp.mean(values * values, axis=-1, keepdims=True) + EPSILON)


def rope_tables(positions, width):
    half_width = width // 2
    inverse = ROPE_BASE ** (-(jnp.arange(half_width, dtype=jnp.float32) * 2.0) / width)
    angles = positions.astype(jnp.float32)[:, None] * inverse[None, :]
    return (jnp.cos(angles), jnp.sin(angles))


def spread_table(table, values):
    half_width = values.shape[-1] // 2
    table_shape = (table.shape[0],) + (1,) * (values.ndim - 2) + (half_width,)
    return table.reshape(table_shape)


def rotate(values, cosine, sine_table):
    half_width = values.shape[-1] // 2
    cosine = spread_table(cosine, values)
    sine_table = spread_table(sine_table, values)
    former = values[..., :half_width]
    latter = values[..., half_width:]
    return jnp.concatenate(
        [former * cosine - latter * sine_table, latter * cosine + former * sine_table], axis=-1
    )


def rotate_back(grads, cosine, sine_table):
    half_width = grads.shape[-1] // 2
    cosine = spread_table(cosine, grads)
    sine_table = spread_table(sine_table, grads)
    former = grads[..., :half_width]
    latter = grads[..., half_width:]
    return jnp.concatenate(
        [former * cosine + latter * sine_table, latter * cosine - former * sine_table], axis=-1
    )


def norm_back(upstream, normed, inverse):
    return inverse * (upstream - normed * jnp.mean(upstream * normed, axis=-1, keepdims=True))


def contract_last(operand_left, operand_right):
    return lax.dot_general(
        operand_left, operand_right, (((1,), (1,)), ((), ())), preferred_element_type=jnp.float32
    )


def contract_rows(operand_left, operand_right):
    return lax.dot_general(
        operand_left, operand_right, (((0,), (0,)), ((), ())), preferred_element_type=jnp.float32
    )


def exchange_kernel(axis, n, gather_count, scatter_count, *refs):
    half = n // 2
    position = 0

    def take(count):
        nonlocal position
        taken = refs[position : position + count]
        position += count
        return taken

    shards, parts = take(gather_count), take(scatter_count)
    wholes, totals = take(gather_count), take(scatter_count)
    from_pair, from_peer = take(scatter_count), take(scatter_count)
    gather_sems = take(5) if gather_count else None
    scatter_sems = take(4) if scatter_count else None

    me = lax.axis_index(axis)
    parity = lax.rem(me, 2)
    group = me // 2
    pair = me + 1 - 2 * parity

    def peer(shift):
        return lax.rem(group + shift, half) * 2 + parity

    barrier = pltpu.get_barrier_semaphore()
    for other in [pair] + [peer(shift) for shift in range(1, half)]:
        pl.semaphore_signal(barrier, inc=1, device_id={axis: other}, device_id_type=MESH)
    pl.semaphore_wait(barrier, half)

    def push(source, target, send, receive, other):
        return pltpu.make_async_remote_copy(
            src_ref=source,
            dst_ref=target,
            send_sem=send,
            recv_sem=receive,
            device_id={axis: other},
            device_id_type=MESH,
        )

    pending = []
    first = {}
    for index in range(scatter_count):
        send_pair, recv_pair, send_peer, recv_peer = scatter_sems
        for shift in list(range(1, half)) + [0]:
            wanted = lax.rem(group + shift, half) * 2 + 1 - parity
            first[index, shift] = push(
                parts[index].at[wanted],
                from_pair[index].at[shift],
                send_pair.at[index, shift],
                recv_pair.at[index, shift],
                pair,
            )
            first[index, shift].start()
    direct = {}
    for index in range(gather_count):
        own_sem, send_peer_g, recv_peer_g, send_pair_g, recv_pair_g = gather_sems
        own = pltpu.make_async_copy(shards[index], wholes[index].at[me], own_sem.at[index])
        own.start()
        pending.append(own.wait)
        for shift in range(1, half):
            direct[index, shift] = push(
                shards[index],
                wholes[index].at[me],
                send_peer_g.at[index, shift],
                recv_peer_g.at[index, shift],
                peer(shift),
            )
            direct[index, shift].start()
        across = push(
            shards[index],
            wholes[index].at[me],
            send_pair_g.at[index, 0],
            recv_pair_g.at[index, 0],
            pair,
        )
        across.start()
        pending.append(across.wait)
    second = {}
    for index in range(scatter_count):
        rows = parts[index].shape[1]
        chunk = min(rows, 32)
        for shift in list(range(1, half)) + [0]:
            first[index, shift].wait_recv()
            kept = peer(shift)

            def add_pair(step, unused, index=index, shift=shift, kept=kept, chunk=chunk):
                span = pl.ds(pl.multiple_of(step * chunk, chunk), chunk)
                summed = parts[index][kept, span, :].astype(jnp.float32) + from_pair[index][
                    shift, span, :
                ].astype(jnp.float32)
                if shift:
                    from_pair[index][shift, span, :] = summed.astype(jnp.bfloat16)
                else:
                    totals[index][span, :] = summed
                return unused

            lax.fori_loop(0, rows // chunk, add_pair, 0)
            if shift:
                second[index, shift] = push(
                    from_pair[index].at[shift],
                    from_peer[index].at[shift - 1],
                    send_peer.at[index, shift],
                    recv_peer.at[index, shift],
                    peer(shift),
                )
                second[index, shift].start()
    for index in range(gather_count):
        for shift in range(1, half):
            direct[index, shift].wait_recv()
            origin = lax.rem(group + half - shift, half) * 2 + parity
            onward = push(
                wholes[index].at[origin],
                wholes[index].at[origin],
                send_pair_g.at[index, shift],
                recv_pair_g.at[index, shift],
                pair,
            )
            onward.start()
            pending.append(direct[index, shift].wait_send)
            pending.append(onward.wait)
    for index in range(scatter_count):
        rows = parts[index].shape[1]
        chunk = min(rows, 32)
        for shift in range(1, half):
            second[index, shift].wait_recv()

        def add_peers(step, unused, index=index, chunk=chunk):
            span = pl.ds(pl.multiple_of(step * chunk, chunk), chunk)
            summed = totals[index][span, :]
            for shift in range(1, half):
                summed += from_peer[index][shift - 1, span, :].astype(jnp.float32)
            totals[index][span, :] = summed
            return unused

        lax.fori_loop(0, rows // chunk, add_peers, 0)
        for shift in range(half):
            pending.append(first[index, shift].wait_send)
            if shift:
                pending.append(second[index, shift].wait_send)
    for wait in pending:
        wait()


def exchange(axis, gathers, scatters, number):
    n = lax.axis_size(axis)
    half = n // 2
    split = [part.reshape((n, part.shape[0] // n) + part.shape[1:]) for part in scatters]
    anywhere = pl.BlockSpec(memory_space=pl.ANY)
    vmem = pl.BlockSpec(memory_space=pltpu.VMEM)
    dma = pltpu.SemaphoreType.DMA
    scratch = [pltpu.VMEM((half,) + part.shape[1:], part.dtype) for part in split]
    scratch += [pltpu.VMEM((half - 1,) + part.shape[1:], part.dtype) for part in split]
    if gathers:
        scratch += [dma((len(gathers),))] + [dma((len(gathers), half))] * 4
    if scatters:
        scratch += [dma((len(scatters), half))] * 4
    results = pl.pallas_call(
        functools.partial(exchange_kernel, axis, n, len(gathers), len(scatters)),
        out_shape=[jax.ShapeDtypeStruct((n,) + shard.shape, shard.dtype) for shard in gathers]
        + [jax.ShapeDtypeStruct(part.shape[1:], jnp.float32) for part in split],
        in_specs=[anywhere] * len(gathers) + [vmem] * len(split),
        out_specs=[anywhere] * len(gathers) + [vmem] * len(split),
        scratch_shapes=scratch,
        compiler_params=pltpu.CompilerParams(
            collective_id=number,
            has_side_effects=True,
            vmem_limit_bytes=(48 if scatters else 4) * 1024 * 1024,
        ),
    )(*gathers, *split)
    count = len(gathers)
    return [
        whole.reshape((n * shard.shape[0],) + shard.shape[1:])
        for whole, shard in zip(results[:count], gathers)
    ] + list(results[count:])


def step_length(length):
    return math.gcd(length, KEY_SPAN)


def allowed_mask(key_pos, query_pos, query_start):
    key_row = key_pos[None, None, None, :]
    return jnp.logical_and(
        key_row <= query_pos[None, None, :, None], key_row >= query_start[None, None, :, None]
    )


def outside(key_pos, query_pos, query_start):
    return jnp.logical_or(
        jnp.min(key_pos) > jnp.max(query_pos), jnp.max(key_pos) < jnp.min(query_start)
    )


def attend_block(
    carried, keys_part, values_part, key_pos, queries, query_pos, query_start, score_scale
):

    def attend_work(current):
        row_top, row_total, mixed_sum = current
        scores = (
            jnp.einsum("qgjd,kgd->gjqk", queries, keys_part, preferred_element_type=jnp.float32)
            * score_scale
        )
        allowed = allowed_mask(key_pos, query_pos, query_start)
        scores = jnp.where(allowed, scores, MASKED)
        new_top = jnp.maximum(row_top, jnp.max(scores, axis=-1))
        probs = jnp.where(allowed, jnp.exp(scores - new_top[..., None]), 0.0)
        factor = jnp.exp(row_top - new_top)
        row_total = row_total * factor + jnp.sum(probs, axis=-1)
        update = jnp.einsum(
            "gjqk,kgd->qgjd",
            probs.astype(jnp.bfloat16),
            values_part,
            preferred_element_type=jnp.float32,
        )
        mixed_sum = mixed_sum * jnp.transpose(factor, (2, 0, 1))[..., None] + update
        return (new_top, row_total, mixed_sum)

    return lax.cond(
        outside(key_pos, query_pos, query_start), lambda current: current, attend_work, carried
    )


def sweep_keys(
    carried, keys_part, values_part, key_pos, queries, query_pos, query_start, score_scale
):
    length = keys_part.shape[0]
    step_len = step_length(length)
    step_count = length // step_len

    def sweep_step(current, pieces):
        return (
            attend_block(
                current,
                pieces[0],
                pieces[1],
                pieces[2],
                queries,
                query_pos,
                query_start,
                score_scale,
            ),
            None,
        )

    stacked = (
        keys_part.reshape((step_count, step_len) + keys_part.shape[1:]),
        values_part.reshape((step_count, step_len) + values_part.shape[1:]),
        key_pos.reshape(step_count, step_len),
    )
    carried, unused = lax.scan(sweep_step, carried, stacked)
    return carried


def score_pair(keys_part, values_part, key_pos, query_side):
    queries, query_pos, query_start, grad_out, delta_rows, log_total, score_scale = query_side
    scores = (
        jnp.einsum("qgjd,kgd->gjqk", queries, keys_part, preferred_element_type=jnp.float32)
        * score_scale
    )
    allowed = allowed_mask(key_pos, query_pos, query_start)
    probs = jnp.where(allowed, jnp.exp(scores - log_total[..., None]), 0.0)
    prob_grad = jnp.einsum(
        "qgjd,kgd->gjqk", grad_out, values_part, preferred_element_type=jnp.float32
    )
    score_grad = probs * (prob_grad - delta_rows[..., None])
    return (probs.astype(jnp.bfloat16), score_grad.astype(jnp.bfloat16))


def stack_steps(all_keys, all_values, all_pos):
    length = all_keys.shape[0]
    step_len = step_length(length)
    step_count = length // step_len
    return (
        all_keys.reshape((step_count, step_len) + all_keys.shape[1:]),
        all_values.reshape((step_count, step_len) + all_values.shape[1:]),
        all_pos.reshape(step_count, step_len),
    )


def attend_back(all_keys, all_values, all_pos, query_side, span_rows):
    queries, query_pos, query_start, grad_out, delta_rows, log_total, score_scale = query_side

    def grad_step(current, pieces):
        keys_part, values_part, key_pos = pieces

        def grad_work(query_acc):
            probs_low, score_low = score_pair(keys_part, values_part, key_pos, query_side)
            query_part = jnp.einsum(
                "gjqk,kgd->qgjd", score_low, keys_part, preferred_element_type=jnp.float32
            )
            value_part = jnp.einsum(
                "gjqk,qgjd->kgd", probs_low, grad_out, preferred_element_type=jnp.float32
            )
            key_part = (
                jnp.einsum("gjqk,qgjd->kgd", score_low, queries, preferred_element_type=jnp.float32)
                * score_scale
            )
            return (
                query_acc + query_part * score_scale,
                jnp.stack([key_part, value_part], axis=1).astype(jnp.bfloat16),
            )

        def skipped(query_acc):
            return (
                query_acc,
                jnp.zeros((keys_part.shape[0], 2) + keys_part.shape[1:], jnp.bfloat16),
            )

        return lax.cond(outside(key_pos, query_pos, query_start), skipped, grad_work, current)

    initial = jnp.zeros(queries.shape, jnp.float32)
    query_grad, terms = lax.scan(grad_step, initial, stack_steps(all_keys, all_values, all_pos))
    return query_grad, terms.reshape(span_rows, -1)


def local(
    tokens,
    positions,
    q_weight,
    k_weight,
    v_weight,
    o_weight,
    gate_weight,
    up_weight,
    down_weight,
    norm1_gain,
    norm2_gain,
    q_gain,
    k_gain,
    cotangent,
):
    head_width = q_gain.shape[0]
    score_scale = head_width ** (-0.5)
    local_heads = q_weight.shape[1] // head_width
    local_groups = k_weight.shape[1] // head_width
    group_size = local_heads // local_groups
    doc_len = positions.shape[0] * lax.axis_size("ctx") // DOCS
    qkv_shard = jnp.concatenate([q_weight, k_weight, v_weight], axis=1)
    pair_shard = jnp.concatenate([gate_weight, up_weight], axis=1)
    inv_first = inv_rms(tokens)
    normed_first = tokens * inv_first
    hidden_first, cot_low = exchange(
        "tp",
        [(normed_first * norm1_gain).astype(jnp.bfloat16), cotangent.astype(jnp.bfloat16)],
        [],
        0,
    )
    block_len = hidden_first.shape[0]
    qkv_full, wo_turned, pair_full, wd_turned, all_pos = exchange(
        "ctx",
        [qkv_shard, o_weight.T, pair_shard, down_weight.T, positions.reshape(-1, 128)],
        [],
        1,
    )
    all_pos = all_pos.reshape(-1)
    local_pos = positions % doc_len
    query_start = positions - local_pos
    cosine, sine_table = rope_tables(local_pos, head_width)
    query_width = local_heads * head_width
    key_width = local_groups * head_width
    raw = jnp.dot(hidden_first, qkv_full, preferred_element_type=jnp.float32)
    query_raw = raw[:, :query_width].reshape(block_len, local_groups, group_size, head_width)
    key_raw = raw[:, query_width : query_width + key_width].reshape(
        block_len, local_groups, head_width
    )
    values_local = raw[:, query_width + key_width :].astype(jnp.bfloat16)
    inv_query = inv_rms(query_raw)
    query_hat = query_raw * inv_query
    queries = rotate(query_hat * q_gain, cosine, sine_table).astype(jnp.bfloat16)
    inv_key = inv_rms(key_raw)
    key_hat = key_raw * inv_key
    keys_local = rotate(key_hat * k_gain, cosine, sine_table).astype(jnp.bfloat16)
    initial = (
        jnp.full((local_groups, group_size, block_len), MASKED, jnp.float32),
        jnp.zeros((local_groups, group_size, block_len), jnp.float32),
        jnp.zeros((block_len, local_groups, group_size, head_width), jnp.float32),
    )
    all_keys, all_values = exchange(
        "ctx", [keys_local.reshape(block_len, key_width), values_local], [], 2
    )
    all_keys = all_keys.reshape(-1, local_groups, head_width)
    all_values = all_values.reshape(-1, local_groups, head_width)
    row_top, row_total, mixed_sum = sweep_keys(
        initial, all_keys, all_values, all_pos, queries, positions, query_start, score_scale
    )
    attended = (mixed_sum / jnp.transpose(row_total, (2, 0, 1))[..., None]).astype(jnp.bfloat16)
    log_total = row_top + jnp.log(row_total)
    attended_flat = attended.reshape(block_len, query_width)
    (projected,) = exchange(
        "tp", [], [contract_last(attended_flat, wo_turned).astype(jnp.bfloat16)], 3
    )
    middle = tokens + projected
    inv_second = inv_rms(middle)
    normed_second = middle * inv_second
    (hidden_second,) = exchange(
        "tp", [(normed_second * norm2_gain).astype(jnp.bfloat16)], [], 4
    )
    unit_count = gate_weight.shape[1]
    gate_up = jnp.dot(hidden_second, pair_full, preferred_element_type=jnp.float32)
    gate = gate_up[:, :unit_count]
    up_proj = gate_up[:, unit_count:]
    sigmoid = jax.nn.sigmoid(gate)
    activation = (gate * sigmoid * up_proj).astype(jnp.bfloat16)
    act_grad = jnp.dot(cot_low, wd_turned, preferred_element_type=jnp.float32)
    gate_grad = (act_grad * up_proj * sigmoid * (1.0 + gate * (1.0 - sigmoid))).astype(jnp.bfloat16)
    up_grad = (act_grad * gate * sigmoid).astype(jnp.bfloat16)
    pair_grad = jnp.concatenate([gate_grad, up_grad], axis=1)
    hidden2_grad, lowered = exchange(
        "tp",
        [],
        [
            contract_last(pair_grad, pair_full).astype(jnp.bfloat16),
            contract_last(activation, wd_turned).astype(jnp.bfloat16),
        ],
        5,
    )
    block_out = middle + lowered
    norm2_part = jnp.sum(hidden2_grad * normed_second, axis=0)
    middle_grad = norm_back(hidden2_grad * norm2_gain, normed_second, inv_second) + cotangent
    (mid_low,) = exchange("tp", [middle_grad.astype(jnp.bfloat16)], [], 6)
    attended_grad = jnp.dot(mid_low, wo_turned, preferred_element_type=jnp.float32).astype(
        jnp.bfloat16
    )
    grad_out = attended_grad.reshape(block_len, local_groups, group_size, head_width)
    delta_rows = jnp.transpose(
        jnp.sum(grad_out.astype(jnp.float32) * attended.astype(jnp.float32), axis=-1), (1, 2, 0)
    )
    query_side = (queries, positions, query_start, grad_out, delta_rows, log_total, score_scale)
    query_grad, key_terms = attend_back(
        all_keys, all_values, all_pos, query_side, block_len * lax.axis_size("ctx")
    )
    (stacked_grads,) = exchange("ctx", [], [key_terms], 7)
    stacked_grads = stacked_grads.reshape(block_len, 2, local_groups, head_width)
    key_grad = stacked_grads[:, 0]
    value_grad = stacked_grads[:, 1]
    query_back = rotate_back(query_grad, cosine, sine_table)
    q_gain_part = jnp.sum(query_back * query_hat, axis=(0, 1, 2))
    query_raw_grad = (
        norm_back(query_back * q_gain, query_hat, inv_query)
        .astype(jnp.bfloat16)
        .reshape(block_len, query_width)
    )
    key_back = rotate_back(key_grad, cosine, sine_table)
    k_gain_part = jnp.sum(key_back * key_hat, axis=(0, 1))
    key_raw_grad = (
        norm_back(key_back * k_gain, key_hat, inv_key)
        .astype(jnp.bfloat16)
        .reshape(block_len, key_width)
    )
    value_low = value_grad.astype(jnp.bfloat16).reshape(block_len, key_width)
    qkv_grad = jnp.concatenate([query_raw_grad, key_raw_grad, value_low], axis=1)
    (hidden1_grad,) = exchange(
        "tp", [], [contract_last(qkv_grad, qkv_full).astype(jnp.bfloat16)], 8
    )
    norm1_part = jnp.sum(hidden1_grad * normed_first, axis=0)
    input_grad = norm_back(hidden1_grad * norm1_gain, normed_first, inv_first) + middle_grad
    gain_parts = jnp.concatenate([norm1_part, norm2_part, q_gain_part, k_gain_part])
    gain_rows = -(-gain_parts.shape[0] // 1024) * 8
    gain_block = jnp.pad(gain_parts, (0, gain_rows * 128 - gain_parts.shape[0])).reshape(
        gain_rows, 128
    )
    (tp_gains,) = exchange("tp", [gain_block], [], 9)
    gain_block = jnp.sum(tp_gains.reshape(-1, gain_rows, 128), axis=0)
    ctx_gains, qkv_wgrad, pair_wgrad, out_wgrad, down_wgrad = exchange(
        "ctx",
        [gain_block],
        [
            contract_rows(hidden_first, qkv_grad).astype(jnp.bfloat16),
            contract_rows(hidden_second, pair_grad).astype(jnp.bfloat16),
            contract_rows(mid_low, attended_flat).astype(jnp.bfloat16),
            contract_rows(cot_low, activation).astype(jnp.bfloat16),
        ],
        10,
    )
    gains = jnp.sum(ctx_gains.reshape(-1, gain_rows, 128), axis=0).reshape(-1)
    width = norm1_gain.shape[0]
    return (
        block_out,
        input_grad,
        qkv_wgrad[:, :query_width],
        qkv_wgrad[:, query_width : query_width + key_width],
        qkv_wgrad[:, query_width + key_width :],
        out_wgrad.T,
        pair_wgrad[:, :unit_count],
        pair_wgrad[:, unit_count:],
        down_wgrad.T,
        gains[:width],
        gains[width : 2 * width],
        gains[2 * width : 2 * width + head_width],
        gains[2 * width + head_width : 2 * width + 2 * head_width],
    )


def solution(mesh):
    in_specs = (
        P(("ctx", "tp"), None),
        P("ctx"),
        P("ctx", "tp"),
        P("ctx", "tp"),
        P("ctx", "tp"),
        P("tp", "ctx"),
        P("ctx", "tp"),
        P("ctx", "tp"),
        P("tp", "ctx"),
        P(),
        P(),
        P(),
        P(),
        P(("ctx", "tp"), None),
    )
    out_specs = (
        P(("ctx", "tp"), None),
        P(("ctx", "tp"), None),
        P("ctx", "tp"),
        P("ctx", "tp"),
        P("ctx", "tp"),
        P("tp", "ctx"),
        P("ctx", "tp"),
        P("ctx", "tp"),
        P("tp", "ctx"),
        P(),
        P(),
        P(),
        P(),
    )
    return jax.shard_map(local, mesh=mesh, in_specs=in_specs, out_specs=out_specs, check_vma=False)
```

time: 1210 us -> 653 us (0.54)
  waiting for transfers between devices: 780 us -> 0 us
  Pallas kernels: 0 us -> 412 us
  blocking collectives: 112 us -> 0 us
  matrix products: 131 us -> 75.6 us
  local copies, waits for them, and re-layouts: 37.4 us -> 67.6 us
  loops' own time: 63.5 us -> 42.7 us
  other arithmetic: 58.9 us -> 43.6 us
  between operations: 15 us -> 1.97 us
    reduce_scatter x10 -> x0, waiting for transfers between devices: 415 us -> none  [the longest x4 81 us: row_sums(): lax.psum_scatter(summed.astype(jnp.bfloat16), 'tp', scatter_dimension=0,...]
    pallas_call x0 -> x11, Pallas kernels: none -> 412 us  [exchange(): pl.pallas_call(functools.partial(exchange_kernel, axis, n, len(gathers),...]
    all_gather x11 -> x0, waiting for transfers between devices: 251 us -> none  [the longest x4 50 us: gather_rows(): return lax.all_gather(part_rows, 'tp', axis=0, tiled=True)]
    unnamed x25 -> x0, waiting for transfers between devices: 114 us -> none
    all_gather x3 -> x0, blocking collectives: 73.1 us -> none  [the longest x1 27.3 us: local(): lax.all_gather(k_weight, 'ctx', axis=0, tiled=True)]
    psum x1 -> x0, blocking collectives: 39.1 us -> none  [local(): lax.psum((norm1_part, norm2_part, q_gain_part, k_gain_part), ('ctx', 'tp'))]
    dot_general x13 -> x16, matrix products: 44.2 us -> 22.8 us  [the longest x4 9.79 us: score_pair(): jnp.einsum('qgjd,kgd->gjqk', grad_out, values_part, preferred_element_typ...]
    another operation x18 -> x9, loops' own time: 42.1 us -> 21.3 us  [the longest x1 20.9 us: attend_back(): lax.scan(grad_step, initial, stack_steps(all_keys, all_values, all_pos))]
  transfers between devices with their start and end apart: 23 -> 0, of which waited for: 19 -> 0; matrix products, arithmetic and copies ran while one was open for 13% -> 0% of each run, Pallas kernels for 0% -> 0%
where the time goes in v1:
time: 653 us; the launch traced here: 644 us
  Pallas kernels  412 us (63%)
  matrix products  75.6 us (12%)
  local copies, waits for them, and re-layouts  67.6 us (10%)
  other arithmetic  43.6 us (7%)
  loops' own time  42.7 us (7%)
    pallas_call x11, Pallas kernels, exchange(): pl.pallas_call(functools.partial(exchange_kernel, axis, n, len(gathers),...  412 us
    another operation x1, loops' own time, sweep_keys(): carried, unused = lax.scan(sweep_step, carried, stacked)  21.2 us
    another operation x1, loops' own time, attend_back(): lax.scan(grad_step, initial, stack_steps(all_keys, all_values, all_pos))  20.9 us
    dot_general x4, matrix products, attend_work(): jnp.einsum('gjqk,kgd->qgjd', probs.astype(jnp.bfloat16), values_part, pre...  15.7 us

profile of v1, /device:TPU:9, one launch (start us, length us, event | category | flops | bytes accessed | tf_op | source)
XLA Modules:
  0.0 643.8 jit_solution(629496386020608318)
XLA Ops:
  4.9 103.4 %shard_map.237 = (bf16[8,128,1024]{2,1,0:T(8,128)(2,1)S(1)}, bf16[8,128,512]{2,1,0:T(8,128)(2,1)S(1)}, bf16[8,128,1536]{2,1,0:T(8,128)(2,1)S(1)}, bf16[8,128,768]{2,1,0:T(8,128)(2,1)S(1)}, s32[8,4,128]{2,1,0:T(4,128)S(1)}) custom-call(bf16[128,1024]{1,0:T(8,128)(2,1)S(1)} %pad_maximum_fusion.11.refs_0_, bf16[128,512]{1,0:T(8,128)(2,1)S(1)} %bitcast.233, ...), custom_call_target="tpu_custom_call" | custom-call | tf_op jit(solution)/shard_map/pallas_call | solution.py:232
  111.9 16.4 %shard_map.238 = (bf16[4,128,1024]{2,1,0:T(8,128)(2,1)S(1)}, bf16[4,128,1024]{2,1,0:T(8,128)(2,1)S(1)}) custom-call(bf16[128,1024]{1,0:T(8,128)(2,1)S(1)} %multiply_convert_fusion.5.refs_0_, bf16[128,1024]{1,0:T(8,128)(2,1)S(1)} %convert_element_type.114.refs_1_), custom_call_target="tpu_custom_call" | custom-call | tf_op jit(solution)/shard_map/pallas_call | solution.py:232
  139.0 67.5 %shard_map.239 = (bf16[8,512,256]{2,1,0:T(8,128)(2,1)S(1)}, bf16[8,512,256]{2,1,0:T(8,128)(2,1)S(1)}) custom-call(bf16[512,256]{1,0:T(8,128)(2,1)S(1)} %bitcast.231, bf16[512,256]{1,0:T(8,128)(2,1)S(1)} %slice.164.refs_1_), custom_call_target="tpu_custom_call" | custom-call | tf_op jit(solution)/shard_map/pallas_call | solution.py:232
  219.7 55.1 %while.31 = (s32[]{:T(128)}, f32[2,2,512]{2,1,0:T(2,128)S(1)}, f32[2,2,512]{2,1,0:T(2,128)S(1)}, f32[512,2,2,128]{3,0,2,1:T(8,128)}, s32[8,512]{1,0:T(8,128)S(1)...) while((s32[]{:T(128)}, f32[2,2,512]{2,1,0:T(2,128)S(1)}, ...), condition=%wide.region_12.13_spmd, body=%wide.region_5.12_spmd.sunk | while | flops 551820288 | bytes 16919844 | solution.py:326
  223.1 7.1 %conditional.4 = (f32[2,2,512]{2,1,0:T(2,128)S(1)}, f32[2,2,512]{2,1,0:T(2,128)S(1)}, f32[512,2,2,128]{3,0,2,1:T(8,128)}) conditional(s32[]{:T(128)} %convert_element_type.175, (s32[1,512]{1,0:T(1,128)S(1)}, s32[512]{0:T(512)S(1)}, s32[512]{0:T(512)S(1)}, bf16[8,512,2,128]{3,1,2,0:T(8,128)(2,1)}, s32[]{:T(128)}, ...), branch_computations={%region_8.10_spmd, %region_11.11_spmd} | conditional | flops 551819264 | bytes 16899096 | solution.py:294
  225.2 3.9 fusion.9
  236.8 7.1 %conditional.4 = (f32[2,2,512]{2,1,0:T(2,128)S(1)}, f32[2,2,512]{2,1,0:T(2,128)S(1)}, f32[512,2,2,128]{3,0,2,1:T(8,128)}) conditional(s32[]{:T(128)} %convert_element_type.175, (s32[1,512]{1,0:T(1,128)S(1)}, s32[512]{0:T(512)S(1)}, s32[512]{0:T(512)S(1)}, bf16[8,512,2,128]{3,1,2,0:T(8,128)(2,1)}, s32[]{:T(128)}, ...), branch_computations={%region_8.10_spmd, %region_11.11_spmd} | conditional | flops 551819264 | bytes 16899096 | solution.py:294
  247.2 7.1 %conditional.4 = (f32[2,2,512]{2,1,0:T(2,128)S(1)}, f32[2,2,512]{2,1,0:T(2,128)S(1)}, f32[512,2,2,128]{3,0,2,1:T(8,128)}) conditional(s32[]{:T(128)} %convert_element_type.175, (s32[1,512]{1,0:T(1,128)S(1)}, s32[512]{0:T(512)S(1)}, s32[512]{0:T(512)S(1)}, bf16[8,512,2,128]{3,1,2,0:T(8,128)(2,1)}, s32[]{:T(128)}, ...), branch_computations={%region_8.10_spmd, %region_11.11_spmd} | conditional | flops 551819264 | bytes 16899096 | solution.py:294
  260.9 7.1 %conditional.4 = (f32[2,2,512]{2,1,0:T(2,128)S(1)}, f32[2,2,512]{2,1,0:T(2,128)S(1)}, f32[512,2,2,128]{3,0,2,1:T(8,128)}) conditional(s32[]{:T(128)} %convert_element_type.175, (s32[1,512]{1,0:T(1,128)S(1)}, s32[512]{0:T(512)S(1)}, s32[512]{0:T(512)S(1)}, bf16[8,512,2,128]{3,1,2,0:T(8,128)(2,1)}, s32[]{:T(128)}, ...), branch_computations={%region_8.10_spmd, %region_11.11_spmd} | conditional | flops 551819264 | bytes 16899096 | solution.py:294
  279.5 10.3 %shard_map.240 = f32[128,1024]{1,0:T(8,128)S(1)} custom-call(bf16[4,128,1024]{2,1,0:T(8,128)(2,1)S(1)} %bitcast.228), custom_call_target="tpu_custom_call" | custom-call | tf_op jit(solution)/shard_map/pallas_call | solution.py:232
  290.1 10.1 %shard_map.241 = bf16[4,128,1024]{2,1,0:T(8,128)(2,1)S(1)} custom-call(bf16[128,1024]{1,0:T(8,128)(2,1)S(1)} %multiply_convert_fusion.4.refs_0_), custom_call_target="tpu_custom_call" | custom-call | tf_op jit(solution)/shard_map/pallas_call | solution.py:232
  310.0 15.5 %shard_map.242 = (f32[128,1024]{1,0:T(8,128)S(1)}, f32[128,1024]{1,0:T(8,128)S(1)}) custom-call(bf16[4,128,1024]{2,1,0:T(8,128)(2,1)S(1)} %bitcast.230, bf16[4,128,1024]{2,1,0:T(8,128)(2,1)S(1)} %bitcast.229), custom_call_target="tpu_custom_call" | custom-call | tf_op jit(solution)/shard_map/pallas_call | solution.py:232
  327.5 10.2 %shard_map.243 = bf16[4,128,1024]{2,1,0:T(8,128)(2,1)S(1)} custom-call(bf16[128,1024]{1,0:T(8,128)(2,1)S(1)} %get-tuple-element.759.refs_0_), custom_call_target="tpu_custom_call" | custom-call | tf_op jit(solution)/shard_map/pallas_call | solution.py:232
  339.5 70.6 %while.32 = (s32[]{:T(128)}, f32[512,2,2,128]{3,0,2,1:T(8,128)S(1)}, bf16[8,512,2,2,128]{4,3,2,1,0:T(2,128)(2,1)}, s32[8,512]{1,0:T(8,128)S(1)}, s32[]{:T(128)},...) while((s32[]{:T(128)}, ...), condition=%wide.region_21.22_spmd, body=%wide.region_16.21_spmd.sunk | while | flops 1354630144 | bytes 29397304 | solution.py:388
  342.8 8.4 %conditional.5 = (f32[512,2,2,128]{3,0,2,1:T(8,128)S(1)}, bf16[1,512,2,2,128]{4,1,3,2,0:T(8,128)(2,1)S(1)}) conditional(s32[]{:T(128)} %convert_element_type.176, (s32[1,512]{1,0:T(1,128)S(1)}, s32[512]{0:T(512)S(1)}, s32[512]{0:T(512)S(1)}, bf16[8,512,2,128]{3,1,2,0:T(8,128)(2,1)}, s32[]{:T(128)}, ...), branch_computations={%region_19.19_spmd, %region_20.20_spmd} | conditional | flops 1354629120 | bytes 28343852 | solution.py:385
  360.4 8.4 %conditional.5 = (f32[512,2,2,128]{3,0,2,1:T(8,128)S(1)}, bf16[1,512,2,2,128]{4,1,3,2,0:T(8,128)(2,1)S(1)}) conditional(s32[]{:T(128)} %convert_element_type.176, (s32[1,512]{1,0:T(1,128)S(1)}, s32[512]{0:T(512)S(1)}, s32[512]{0:T(512)S(1)}, bf16[8,512,2,128]{3,1,2,0:T(8,128)(2,1)}, s32[]{:T(128)}, ...), branch_computations={%region_19.19_spmd, %region_20.20_spmd} | conditional | flops 1354629120 | bytes 28343852 | solution.py:385
  373.4 8.4 %conditional.5 = (f32[512,2,2,128]{3,0,2,1:T(8,128)S(1)}, bf16[1,512,2,2,128]{4,1,3,2,0:T(8,128)(2,1)S(1)}) conditional(s32[]{:T(128)} %convert_element_type.176, (s32[1,512]{1,0:T(1,128)S(1)}, s32[512]{0:T(512)S(1)}, s32[512]{0:T(512)S(1)}, bf16[8,512,2,128]{3,1,2,0:T(8,128)(2,1)}, s32[]{:T(128)}, ...), branch_computations={%region_19.19_spmd, %region_20.20_spmd} | conditional | flops 1354629120 | bytes 28343852 | solution.py:385
  391.0 8.4 %conditional.5 = (f32[512,2,2,128]{3,0,2,1:T(8,128)S(1)}, bf16[1,512,2,2,128]{4,1,3,2,0:T(8,128)(2,1)S(1)}) conditional(s32[]{:T(128)} %convert_element_type.176, (s32[1,512]{1,0:T(1,128)S(1)}, s32[512]{0:T(512)S(1)}, s32[512]{0:T(512)S(1)}, bf16[8,512,2,128]{3,1,2,0:T(8,128)(2,1)}, s32[]{:T(128)}, ...), branch_computations={%region_19.19_spmd, %region_20.20_spmd} | conditional | flops 1354629120 | bytes 28343852 | solution.py:385
  426.2 4.1 multiply_reduce_fusion
  430.3 7.2 %reshape_reshape.3.refs_0_ = bf16[8,512,512]{2,1,0:T(8,128)(2,1)} reshape(bf16[8,512,2,2,128]{4,3,2,1,0:T(2,128)(2,1)} %get-tuple-element.451) | data formatting | bytes 8388608 | tf_op jit(solution)/shard_map/reshape;reshape | solution.py:222
  439.8 62.1 %shard_map.244 = f32[512,512]{1,0:T(8,128)S(1)} custom-call(bf16[8,512,512]{2,1,0:T(8,128)(2,1)S(1)} %copy-done), custom_call_target="tpu_custom_call" | custom-call | tf_op jit(solution)/shard_map/pallas_call | solution.py:232
  517.3 10.2 %shard_map.245 = f32[128,1024]{1,0:T(8,128)S(1)} custom-call(bf16[4,128,1024]{2,1,0:T(8,128)(2,1)S(1)} %bitcast.227), custom_call_target="tpu_custom_call" | custom-call | tf_op jit(solution)/shard_map/pallas_call | solution.py:232
  528.3 4.9 shard_map.246
  535.4 101.7 %shard_map.247 = (f32[8,24,128]{2,1,0:T(8,128)S(1)}, f32[128,1024]{1,0:T(8,128)S(1)}, f32[128,1536]{1,0:T(8,128)S(1)}, f32[128,512]{1,0:T(8,128)S(1)}, f32[128,768]{1,0:T(8,128)S(1)}) custom-call(f32[24,128]{1,0:T(8,128)S(1)} %reduce_sum.177.refs_0_, bf16[8,128,1024]{2,1,0:T(8,128)(2,1)} %bitcast.252, bf16[8,128,1536]{2,1,0:T(8,128)(2,1)} %bitcast.249, ...), custom_call_target="tpu_custom_call" | custom-call | tf_op jit(solution)/shard_map/pallas_call | solution.py:232
  (286 shorter events, 172.1 us)
Async XLA Ops:
  0.6 110.3 %copy-start.14 = (f32[128,1024]{1,0:T(8,128)S(1)}, f32[128,1024]{1,0:T(8,128)}, u32[]{:S(2)}) copy-start(f32[128,1024]{1,0:T(8,128)} %param.22) | copy-start | bytes 1572868
  0.7 111.0 %copy-start.33 = (f32[1024]{0:T(1024)S(1)}, f32[1024]{0:T(1024)}, u32[]{:S(2)}) copy-start(f32[1024]{0:T(1024)} %param.31) | copy-start | bytes 12292
  4.9 107.0 %copy-start.24 = (f32[128,1024]{1,0:T(8,128)S(1)}, f32[128,1024]{1,0:T(8,128)}, u32[]{:S(2)}) copy-start(f32[128,1024]{1,0:T(8,128)} %param.35) | copy-start | bytes 1572868
  111.0 20.9 %copy-start.3 = (bf16[8,128,1024]{2,1,0:T(8,128)(2,1)}, bf16[8,128,1024]{2,1,0:T(8,128)(2,1)S(1)}, u32[]{:S(2)}) copy-start(bf16[8,128,1024]{2,1,0:T(8,128)(2,1)S(1)} %get-tuple-element.438) | copy-start | bytes 6291460
  133.3 3.9 copy-start.17
  136.3 73.1 %copy-start.19 = (f32[512,64]{1,0:T(8,128)}, f32[512,64]{1,0:T(8,128)S(1)}, u32[]{:S(2)}) copy-start(f32[512,64]{1,0:T(8,128)S(1)} %get-tuple-element.792) | copy-start | bytes 393220
  211.8 5.6 copy-start.36
  213.7 4.1 copy-start.12
  213.7 4.1 copy-start.20
  274.7 4.0 copy-start.11
  278.7 58.9 %copy-start.27 = (bf16[512,2,2,128]{0,3,2,1:T(8,128)(2,1)}, bf16[512,2,2,128]{0,3,2,1:T(8,128)(2,1)S(1)}, u32[]{:S(2)}) copy-start(bf16[512,2,2,128]{0,3,2,1:T(8,128)(2,1)S(1)} %divide_convert_fusion) | copy-start | bytes 1572868
  278.7 11.1 %copy-start.15 = (f32[128,1024]{1,0:T(8,128)S(1)}, f32[128,1024]{1,0:T(8,128)}, u32[]{:S(2)}) copy-start(f32[128,1024]{1,0:T(8,128)} %param.22) | copy-start | bytes 1572868
  279.5 10.5 %copy-start.32 = (f32[1024]{0:T(1024)S(1)}, f32[1024]{0:T(1024)}, u32[]{:S(2)}) copy-start(f32[1024]{0:T(1024)} %param.32) | copy-start | bytes 12292
  289.8 10.4 %copy-start.2 = (bf16[8,128,1536]{2,1,0:T(8,128)(2,1)S(1)}, bf16[8,128,1536]{2,1,0:T(8,128)(2,1)}, u32[]{:S(2)}) copy-start(bf16[8,128,1536]{2,1,0:T(8,128)(2,1)} %copy-done.1) | copy-start | bytes 9437188
  303.6 3.6 copy-start.42
  310.0 16.3 %copy-start.25 = (f32[128,1024]{1,0:T(8,128)S(1)}, f32[128,1024]{1,0:T(8,128)}, u32[]{:S(2)}) copy-start(f32[128,1024]{1,0:T(8,128)} %param.35) | copy-start | bytes 1572868
  515.9 11.6 %copy-start.16 = (f32[128,1024]{1,0:T(8,128)S(1)}, f32[128,1024]{1,0:T(8,128)}, u32[]{:S(2)}) copy-start(f32[128,1024]{1,0:T(8,128)} %param.22) | copy-start | bytes 1572868
  515.9 11.6 %copy-start.38 = (f32[128]{0:T(128)S(1)}, f32[128]{0:T(128)}, u32[]{:S(2)}) copy-start(f32[128]{0:T(128)} %copy-done.37) | copy-start | bytes 1540
  517.2 11.0 %copy-start.35 = (f32[512]{0:T(512)S(1)}, f32[512]{0:T(512)}, u32[]{:S(2)}) copy-start(f32[512]{0:T(512)} %get-tuple-element.769) | copy-start | bytes 6148
  517.2 11.1 %copy-start.34 = (f32[1024]{0:T(1024)S(1)}, f32[1024]{0:T(1024)}, u32[]{:S(2)}) copy-start(f32[1024]{0:T(1024)} %get-tuple-element.697) | copy-start | bytes 12292
  517.3 16.0 %copy-start.7 = (bf16[4,128,1024]{2,1,0:T(8,128)(2,1)S(1)}, bf16[4,128,1024]{2,1,0:T(8,128)(2,1)}, u32[]{:S(2)}) copy-start(bf16[4,128,1024]{2,1,0:T(8,128)(2,1)} %copy-done.5) | copy-start | bytes 3145732
  637.1 5.3 copy-start.41
  637.1 5.3 copy-start.26
  637.1 5.3 copy-start.39
  (22 other events, 43.1 us)

commit v2 on v1

v2 whole, which is shorter than its diff:
```python
import functools

import jax
import jax.numpy as jnp
from jax import lax
from jax.experimental import pallas as pl
from jax.experimental.pallas import tpu as pltpu
from jax.sharding import PartitionSpec as P

DOCS = 2


EPSILON = 1e-06
ROPE_BASE = 1000000.0
MASKED = -1e30
MESH = pl.DeviceIdType.MESH


def inv_rms(values):
    return lax.rsqrt(jnp.mean(values * values, axis=-1, keepdims=True) + EPSILON)


def rope_tables(positions, width):
    half_width = width // 2
    inverse = ROPE_BASE ** (-(jnp.arange(half_width, dtype=jnp.float32) * 2.0) / width)
    angles = positions.astype(jnp.float32)[:, None] * inverse[None, :]
    return (jnp.cos(angles), jnp.sin(angles))


def spread_table(table, values):
    half_width = values.shape[-1] // 2
    table_shape = (table.shape[0],) + (1,) * (values.ndim - 2) + (half_width,)
    return table.reshape(table_shape)


def rotate(values, cosine, sine_table):
    half_width = values.shape[-1] // 2
    cosine = spread_table(cosine, values)
    sine_table = spread_table(sine_table, values)
    former = values[..., :half_width]
    latter = values[..., half_width:]
    return jnp.concatenate(
        [former * cosine - latter * sine_table, latter * cosine + former * sine_table], axis=-1
    )


def rotate_back(grads, cosine, sine_table):
    half_width = grads.shape[-1] // 2
    cosine = spread_table(cosine, grads)
    sine_table = spread_table(sine_table, grads)
    former = grads[..., :half_width]
    latter = grads[..., half_width:]
    return jnp.concatenate(
        [former * cosine + latter * sine_table, latter * cosine - former * sine_table], axis=-1
    )


def norm_back(upstream, normed, inverse):
    return inverse * (upstream - normed * jnp.mean(upstream * normed, axis=-1, keepdims=True))


def contract_last(operand_left, operand_right):
    return lax.dot_general(
        operand_left, operand_right, (((1,), (1,)), ((), ())), preferred_element_type=jnp.float32
    )


def contract_rows(operand_left, operand_right):
    return lax.dot_general(
        operand_left, operand_right, (((0,), (0,)), ((), ())), preferred_element_type=jnp.float32
    )


class Line:
    def __init__(self, axis, n):
        self.axis, self.half = axis, n // 2
        self.me = lax.axis_index(axis)
        self.parity = lax.rem(self.me, 2)
        self.group = self.me // 2
        self.pair = self.me + 1 - 2 * self.parity

    def peer(self, shift):
        return lax.rem(self.group + shift, self.half) * 2 + self.parity


def exchange_kernel(gather_axes, scatter_axes, sizes, *refs):
    gather_count, scatter_count = len(gather_axes), len(scatter_axes)
    position = 0

    def take(count):
        nonlocal position
        taken = refs[position : position + count]
        position += count
        return taken

    shards, parts = take(gather_count), take(scatter_count)
    wholes, totals = take(gather_count), take(scatter_count)
    from_pair, from_peer = take(scatter_count), take(scatter_count)
    gather_sems = take(5) if gather_count else None
    scatter_sems = take(4) if scatter_count else None
    lines = {axis: Line(axis, n) for axis, n in sizes.items()}

    barrier = pltpu.get_barrier_semaphore()
    for axis, line in lines.items():
        for other in [line.pair] + [line.peer(shift) for shift in range(1, line.half)]:
            pl.semaphore_signal(barrier, inc=1, device_id={axis: other}, device_id_type=MESH)
    pl.semaphore_wait(barrier, sum(line.half for line in lines.values()))

    def push(source, target, send, receive, axis, other):
        return pltpu.make_async_remote_copy(
            src_ref=source,
            dst_ref=target,
            send_sem=send,
            recv_sem=receive,
            device_id={axis: other},
            device_id_type=MESH,
        )

    pending = []
    first = {}
    for index in range(scatter_count):
        line = lines[scatter_axes[index]]
        half, group, parity = line.half, line.group, line.parity
        send_pair, recv_pair, send_peer, recv_peer = scatter_sems
        for shift in list(range(1, half)) + [0]:
            wanted = lax.rem(group + shift, half) * 2 + 1 - parity
            first[index, shift] = push(
                parts[index].at[wanted],
                from_pair[index].at[shift],
                send_pair.at[index, shift],
                recv_pair.at[index, shift],
                line.axis,
                line.pair,
            )
            first[index, shift].start()
    direct = {}
    for index in range(gather_count):
        line = lines[gather_axes[index]]
        half, group, parity, me = line.half, line.group, line.parity, line.me
        own_sem, send_peer_g, recv_peer_g, send_pair_g, recv_pair_g = gather_sems
        own = pltpu.make_async_copy(shards[index], wholes[index].at[me], own_sem.at[index])
        own.start()
        pending.append(own.wait)
        for shift in range(1, half):
            direct[index, shift] = push(
                shards[index],
                wholes[index].at[me],
                send_peer_g.at[index, shift],
                recv_peer_g.at[index, shift],
                line.axis,
                line.peer(shift),
            )
            direct[index, shift].start()
        across = push(
            shards[index],
            wholes[index].at[me],
            send_pair_g.at[index, 0],
            recv_pair_g.at[index, 0],
            line.axis,
            line.pair,
        )
        across.start()
        pending.append(across.wait)
    second = {}
    for index in range(scatter_count):
        line = lines[scatter_axes[index]]
        half, group, parity = line.half, line.group, line.parity
        rows = parts[index].shape[1]
        chunk = min(rows, 32)
        for shift in list(range(1, half)) + [0]:
            first[index, shift].wait_recv()
            kept = line.peer(shift)

            def add_pair(step, unused, index=index, shift=shift, kept=kept, chunk=chunk):
                span = pl.ds(pl.multiple_of(step * chunk, chunk), chunk)
                summed = parts[index][kept, span, :].astype(jnp.float32) + from_pair[index][
                    shift, span, :
                ].astype(jnp.float32)
                if shift:
                    from_pair[index][shift, span, :] = summed.astype(jnp.bfloat16)
                else:
                    totals[index][span, :] = summed
                return unused

            lax.fori_loop(0, rows // chunk, add_pair, 0)
            if shift:
                second[index, shift] = push(
                    from_pair[index].at[shift],
                    from_peer[index].at[shift - 1],
                    send_peer.at[index, shift],
                    recv_peer.at[index, shift],
                    line.axis,
                    line.peer(shift),
                )
                second[index, shift].start()
    for index in range(gather_count):
        line = lines[gather_axes[index]]
        half, group, parity, me = line.half, line.group, line.parity, line.me
        for shift in range(1, half):
            direct[index, shift].wait_recv()
            origin = lax.rem(group + half - shift, half) * 2 + parity
            onward = push(
                wholes[index].at[origin],
                wholes[index].at[origin],
                send_pair_g.at[index, shift],
                recv_pair_g.at[index, shift],
                line.axis,
                line.pair,
            )
            onward.start()
            pending.append(direct[index, shift].wait_send)
            pending.append(onward.wait)
    for index in range(scatter_count):
        line = lines[scatter_axes[index]]
        half, group, parity = line.half, line.group, line.parity
        rows = parts[index].shape[1]
        chunk = min(rows, 32)
        for shift in range(1, half):
            second[index, shift].wait_recv()

        def add_peers(step, unused, index=index, chunk=chunk, half=half):
            span = pl.ds(pl.multiple_of(step * chunk, chunk), chunk)
            summed = totals[index][span, :]
            for shift in range(1, half):
                summed += from_peer[index][shift - 1, span, :].astype(jnp.float32)
            totals[index][span, :] = summed
            return unused

        lax.fori_loop(0, rows // chunk, add_peers, 0)
        for shift in range(half):
            pending.append(first[index, shift].wait_send)
            if shift:
                pending.append(second[index, shift].wait_send)
    for wait in pending:
        wait()


def exchange(gathers, scatters, number):
    axes = sorted({axis for axis, unused in gathers + scatters})
    sizes = {axis: lax.axis_size(axis) for axis in axes}
    most = max(sizes.values()) // 2
    shards = [shard for unused, shard in gathers]
    split = [
        part.reshape((sizes[axis], part.shape[0] // sizes[axis]) + part.shape[1:])
        for axis, part in scatters
    ]
    anywhere = pl.BlockSpec(memory_space=pl.ANY)
    vmem = pl.BlockSpec(memory_space=pltpu.VMEM)
    dma = pltpu.SemaphoreType.DMA
    scratch = [pltpu.VMEM((part.shape[0] // 2,) + part.shape[1:], part.dtype) for part in split]
    scratch += [
        pltpu.VMEM((part.shape[0] // 2 - 1,) + part.shape[1:], part.dtype) for part in split
    ]
    if gathers:
        scratch += [dma((len(gathers),))] + [dma((len(gathers), most))] * 4
    if scatters:
        scratch += [dma((len(scatters), most))] * 4
    wholes = [
        jax.ShapeDtypeStruct((sizes[axis],) + shard.shape, shard.dtype) for axis, shard in gathers
    ]
    results = pl.pallas_call(
        functools.partial(
            exchange_kernel,
            tuple(axis for axis, unused in gathers),
            tuple(axis for axis, unused in scatters),
            sizes,
        ),
        out_shape=wholes + [jax.ShapeDtypeStruct(part.shape[1:], jnp.float32) for part in split],
        in_specs=[anywhere] * len(gathers) + [vmem] * len(split),
        out_specs=[anywhere] * len(gathers) + [vmem] * len(split),
        scratch_shapes=scratch,
        compiler_params=pltpu.CompilerParams(
            collective_id=number,
            has_side_effects=True,
            vmem_limit_bytes=(48 if scatters else 4) * 1024 * 1024,
        ),
    )(*shards, *split)
    return [
        whole.reshape((-1,) + shard.shape[1:]) for whole, shard in zip(results, shards)
    ] + list(results[len(shards) :])


def turned(operand_left, operand_right):
    return lax.dot_general(
        operand_left, operand_right, (((0,), (0,)), ((), ())), preferred_element_type=jnp.float32
    )


def needed(blocks_ref, own_ref, index, doc_blocks):
    block, own = blocks_ref[index], own_ref[0]
    return jnp.logical_and(block <= own, block >= own - lax.rem(own, doc_blocks))


def attend_kernel(
    scale, heads, groups, doc_blocks, blocks_ref, own_ref, q_ref, k_ref, v_ref, out_ref, log_ref,
    top_ref, total_ref, mixed_ref,
):
    length = q_ref.shape[0]
    width = q_ref.shape[1] // heads
    top_ref[...] = jnp.full_like(top_ref, MASKED)
    total_ref[...] = jnp.zeros_like(total_ref)
    mixed_ref[...] = jnp.zeros_like(mixed_ref)

    def visit(index, unused):
        @pl.when(needed(blocks_ref, own_ref, index, doc_blocks))
        def attend_work():
            ahead = (own_ref[0] - blocks_ref[index]) * length
            rows = pl.ds(pl.multiple_of(index * length, length), length)
            allowed = lax.broadcasted_iota(jnp.int32, (length, length), 1) <= (
                lax.broadcasted_iota(jnp.int32, (length, length), 0) + ahead
            )
            for head in range(heads):
                group = head * groups // heads
                columns = pl.ds(head * width, width)
                shared = pl.ds(group * width, width)
                scores = contract_last(q_ref[:, columns], k_ref[rows, shared]) * scale
                scores = jnp.where(allowed, scores, MASKED)
                old_top = top_ref[head]
                new_top = jnp.maximum(old_top, jnp.max(scores, axis=1, keepdims=True))
                probs = jnp.exp(scores - new_top)
                factor = jnp.exp(old_top - new_top)
                top_ref[head] = new_top
                total_ref[head] = total_ref[head] * factor + jnp.sum(probs, axis=1, keepdims=True)
                mixed_ref[:, columns] = mixed_ref[:, columns] * factor + jnp.dot(
                    probs.astype(jnp.bfloat16), v_ref[rows, shared],
                    preferred_element_type=jnp.float32,
                )

        return unused

    lax.fori_loop(0, k_ref.shape[0] // length, visit, 0)
    for head in range(heads):
        columns = pl.ds(head * width, width)
        out_ref[:, columns] = (mixed_ref[:, columns] / total_ref[head]).astype(out_ref.dtype)
        log_ref[head] = top_ref[head] + jnp.log(total_ref[head])


def attend_back_kernel(
    scale, heads, groups, doc_blocks, blocks_ref, own_ref, q_ref, k_ref, v_ref, grad_ref, log_ref,
    delta_ref, query_ref, terms_ref,
):
    length = q_ref.shape[0]
    width = q_ref.shape[1] // heads
    query_ref[...] = jnp.zeros_like(query_ref)

    def visit(index, unused):
        rows = pl.ds(pl.multiple_of(index * length, length), length)
        used = needed(blocks_ref, own_ref, index, doc_blocks)

        @pl.when(jnp.logical_not(used))
        def skipped():
            terms_ref[rows, :] = jnp.zeros((length, terms_ref.shape[1]), terms_ref.dtype)

        @pl.when(used)
        def grad_work():
            ahead = (own_ref[0] - blocks_ref[index]) * length
            allowed = lax.broadcasted_iota(jnp.int32, (length, length), 0) <= (
                lax.broadcasted_iota(jnp.int32, (length, length), 1) + ahead
            )
            for group in range(groups):
                shared = pl.ds(group * width, width)
                keys_part, values_part = k_ref[rows, shared], v_ref[rows, shared]
                key_sum = value_sum = None
                for head in range(group * heads // groups, (group + 1) * heads // groups):
                    columns = pl.ds(head * width, width)
                    queries, grad_out = q_ref[:, columns], grad_ref[:, columns]
                    scores = contract_last(keys_part, queries) * scale
                    probs = jnp.where(allowed, jnp.exp(scores - log_ref[head]), 0.0)
                    prob_grad = contract_last(values_part, grad_out)
                    score_low = (probs * (prob_grad - delta_ref[head])).astype(jnp.bfloat16)
                    value_part = jnp.dot(
                        probs.astype(jnp.bfloat16), grad_out, preferred_element_type=jnp.float32
                    )
                    key_part = jnp.dot(score_low, queries, preferred_element_type=jnp.float32)
                    key_sum = key_part if key_sum is None else key_sum + key_part
                    value_sum = value_part if value_sum is None else value_sum + value_part
                    query_ref[:, columns] += turned(score_low, keys_part)
                terms_ref[rows, shared] = (key_sum * scale).astype(terms_ref.dtype)
                terms_ref[rows, pl.ds((groups + group) * width, width)] = value_sum.astype(
                    terms_ref.dtype
                )

        return unused

    lax.fori_loop(0, k_ref.shape[0] // length, visit, 0)
    query_ref[...] = query_ref[...] * scale


def attention_call(kernel, settings, inputs, outputs, scratch):
    smem = pl.BlockSpec(memory_space=pltpu.SMEM)
    vmem = pl.BlockSpec(memory_space=pltpu.VMEM)
    return pl.pallas_call(
        functools.partial(kernel, *settings),
        out_shape=outputs,
        in_specs=[smem, smem] + [vmem] * (len(inputs) - 2),
        out_specs=[vmem] * len(outputs),
        scratch_shapes=scratch,
        compiler_params=pltpu.CompilerParams(vmem_limit_bytes=56 * 1024 * 1024),
    )(*inputs)


def local(
    tokens,
    positions,
    q_weight,
    k_weight,
    v_weight,
    o_weight,
    gate_weight,
    up_weight,
    down_weight,
    norm1_gain,
    norm2_gain,
    q_gain,
    k_gain,
    cotangent,
):
    head_width = q_gain.shape[0]
    score_scale = head_width ** (-0.5)
    local_heads = q_weight.shape[1] // head_width
    local_groups = k_weight.shape[1] // head_width
    group_size = local_heads // local_groups
    doc_len = positions.shape[0] * lax.axis_size("ctx") // DOCS
    qkv_shard = jnp.concatenate([q_weight, k_weight, v_weight], axis=1)
    pair_shard = jnp.concatenate([gate_weight, up_weight], axis=1)
    inv_first = inv_rms(tokens)
    normed_first = tokens * inv_first
    qkv_full, hidden_first, cot_low, wo_turned, pair_full, wd_turned, all_pos = exchange(
        [
            ("ctx", qkv_shard),
            ("tp", (normed_first * norm1_gain).astype(jnp.bfloat16)),
            ("tp", cotangent.astype(jnp.bfloat16)),
            ("ctx", o_weight.T),
            ("ctx", pair_shard),
            ("ctx", down_weight.T),
            ("ctx", positions.reshape(-1, 128)),
        ],
        [],
        0,
    )
    block_len = hidden_first.shape[0]
    key_blocks = all_pos.reshape(-1, block_len)[:, 0] // block_len
    own_block = positions[:1] // block_len
    local_pos = positions % doc_len
    query_start = positions - local_pos
    cosine, sine_table = rope_tables(local_pos, head_width)
    query_width = local_heads * head_width
    key_width = local_groups * head_width
    raw = jnp.dot(hidden_first, qkv_full, preferred_element_type=jnp.float32)
    query_raw = raw[:, :query_width].reshape(block_len, local_groups, group_size, head_width)
    key_raw = raw[:, query_width : query_width + key_width].reshape(
        block_len, local_groups, head_width
    )
    values_local = raw[:, query_width + key_width :].astype(jnp.bfloat16)
    inv_query = inv_rms(query_raw)
    query_hat = query_raw * inv_query
    queries = rotate(query_hat * q_gain, cosine, sine_table).astype(jnp.bfloat16)
    inv_key = inv_rms(key_raw)
    key_hat = key_raw * inv_key
    keys_local = rotate(key_hat * k_gain, cosine, sine_table).astype(jnp.bfloat16)
    queries = queries.reshape(block_len, query_width)
    all_keys, all_values = exchange(
        [("ctx", keys_local.reshape(block_len, key_width)), ("ctx", values_local)], [], 2
    )
    settings = (score_scale, local_heads, local_groups, doc_len // block_len)
    attended_flat, log_total = attention_call(
        attend_kernel,
        settings,
        (key_blocks, own_block, queries, all_keys, all_values),
        [
            jax.ShapeDtypeStruct((block_len, query_width), jnp.bfloat16),
            jax.ShapeDtypeStruct((local_heads, block_len, 1), jnp.float32),
        ],
        [
            pltpu.VMEM((local_heads, block_len, 1), jnp.float32),
            pltpu.VMEM((local_heads, block_len, 1), jnp.float32),
            pltpu.VMEM((block_len, query_width), jnp.float32),
        ],
    )
    (projected,) = exchange(
        [], [("tp", contract_last(attended_flat, wo_turned).astype(jnp.bfloat16))], 3
    )
    middle = tokens + projected
    inv_second = inv_rms(middle)
    normed_second = middle * inv_second
    (hidden_second,) = exchange(
        [("tp", (normed_second * norm2_gain).astype(jnp.bfloat16))], [], 4
    )
    unit_count = gate_weight.shape[1]
    gate_up = jnp.dot(hidden_second, pair_full, preferred_element_type=jnp.float32)
    gate = gate_up[:, :unit_count]
    up_proj = gate_up[:, unit_count:]
    sigmoid = jax.nn.sigmoid(gate)
    activation = (gate * sigmoid * up_proj).astype(jnp.bfloat16)
    act_grad = jnp.dot(cot_low, wd_turned, preferred_element_type=jnp.float32)
    gate_grad = (act_grad * up_proj * sigmoid * (1.0 + gate * (1.0 - sigmoid))).astype(jnp.bfloat16)
    up_grad = (act_grad * gate * sigmoid).astype(jnp.bfloat16)
    pair_grad = jnp.concatenate([gate_grad, up_grad], axis=1)
    hidden2_grad, lowered = exchange(
        [],
        [
            ("tp", contract_last(pair_grad, pair_full).astype(jnp.bfloat16)),
            ("tp", contract_last(activation, wd_turned).astype(jnp.bfloat16)),
        ],
        5,
    )
    block_out = middle + lowered
    norm2_part = jnp.sum(hidden2_grad * normed_second, axis=0)
    middle_grad = norm_back(hidden2_grad * norm2_gain, normed_second, inv_second) + cotangent
    (mid_low,) = exchange([("tp", middle_grad.astype(jnp.bfloat16))], [], 6)
    attended_grad = jnp.dot(mid_low, wo_turned, preferred_element_type=jnp.float32).astype(
        jnp.bfloat16
    )
    delta_rows = jnp.sum(
        (attended_grad.astype(jnp.float32) * attended_flat.astype(jnp.float32)).reshape(
            block_len, local_heads, head_width
        ),
        axis=-1,
    )
    query_grad, key_terms = attention_call(
        attend_back_kernel,
        settings,
        (
            key_blocks,
            own_block,
            queries,
            all_keys,
            all_values,
            attended_grad,
            log_total.reshape(local_heads, 1, block_len),
            delta_rows.T.reshape(local_heads, 1, block_len),
        ),
        [
            jax.ShapeDtypeStruct((block_len, query_width), jnp.float32),
            jax.ShapeDtypeStruct((all_keys.shape[0], 2 * key_width), jnp.bfloat16),
        ],
        [],
    )
    query_grad = query_grad.reshape(block_len, local_groups, group_size, head_width)
    (stacked_grads,) = exchange([], [("ctx", key_terms)], 7)
    stacked_grads = stacked_grads.reshape(block_len, 2, local_groups, head_width)
    key_grad = stacked_grads[:, 0]
    value_grad = stacked_grads[:, 1]
    query_back = rotate_back(query_grad, cosine, sine_table)
    q_gain_part = jnp.sum(query_back * query_hat, axis=(0, 1, 2))
    query_raw_grad = (
        norm_back(query_back * q_gain, query_hat, inv_query)
        .astype(jnp.bfloat16)
        .reshape(block_len, query_width)
    )
    key_back = rotate_back(key_grad, cosine, sine_table)
    k_gain_part = jnp.sum(key_back * key_hat, axis=(0, 1))
    key_raw_grad = (
        norm_back(key_back * k_gain, key_hat, inv_key)
        .astype(jnp.bfloat16)
        .reshape(block_len, key_width)
    )
    value_low = value_grad.astype(jnp.bfloat16).reshape(block_len, key_width)
    qkv_grad = jnp.concatenate([query_raw_grad, key_raw_grad, value_low], axis=1)
    (hidden1_grad,) = exchange(
        [], [("tp", contract_last(qkv_grad, qkv_full).astype(jnp.bfloat16))], 8
    )
    norm1_part = jnp.sum(hidden1_grad * normed_first, axis=0)
    input_grad = norm_back(hidden1_grad * norm1_gain, normed_first, inv_first) + middle_grad
    gain_parts = jnp.concatenate([norm1_part, norm2_part, q_gain_part, k_gain_part])
    gain_rows = -(-gain_parts.shape[0] // 1024) * 8
    gain_block = jnp.pad(gain_parts, (0, gain_rows * 128 - gain_parts.shape[0])).reshape(
        gain_rows, 128
    )
    (tp_gains,) = exchange([("tp", gain_block)], [], 9)
    gain_block = jnp.sum(tp_gains.reshape(-1, gain_rows, 128), axis=0)
    ctx_gains, qkv_wgrad, pair_wgrad, out_wgrad, down_wgrad = exchange(
        [("ctx", gain_block)],
        [
            ("ctx", contract_rows(hidden_first, qkv_grad).astype(jnp.bfloat16)),
            ("ctx", contract_rows(hidden_second, pair_grad).astype(jnp.bfloat16)),
            ("ctx", contract_rows(mid_low, attended_flat).astype(jnp.bfloat16)),
            ("ctx", contract_rows(cot_low, activation).astype(jnp.bfloat16)),
        ],
        10,
    )
    gains = jnp.sum(ctx_gains.reshape(-1, gain_rows, 128), axis=0).reshape(-1)
    width = norm1_gain.shape[0]
    return (
        block_out,
        input_grad,
        qkv_wgrad[:, :query_width],
        qkv_wgrad[:, query_width : query_width + key_width],
        qkv_wgrad[:, query_width + key_width :],
        out_wgrad.T,
        pair_wgrad[:, :unit_count],
        pair_wgrad[:, unit_count:],
        down_wgrad.T,
        gains[:width],
        gains[width : 2 * width],
        gains[2 * width : 2 * width + head_width],
        gains[2 * width + head_width : 2 * width + 2 * head_width],
    )


def solution(mesh):
    in_specs = (
        P(("ctx", "tp"), None),
        P("ctx"),
        P("ctx", "tp"),
        P("ctx", "tp"),
        P("ctx", "tp"),
        P("tp", "ctx"),
        P("ctx", "tp"),
        P("ctx", "tp"),
        P("tp", "ctx"),
        P(),
        P(),
        P(),
        P(),
        P(("ctx", "tp"), None),
    )
    out_specs = (
        P(("ctx", "tp"), None),
        P(("ctx", "tp"), None),
        P("ctx", "tp"),
        P("ctx", "tp"),
        P("ctx", "tp"),
        P("tp", "ctx"),
        P("ctx", "tp"),
        P("ctx", "tp"),
        P("tp", "ctx"),
        P(),
        P(),
        P(),
        P(),
    )
    return jax.shard_map(local, mesh=mesh, in_specs=in_specs, out_specs=out_specs, check_vma=False)
```

time: 653 us -> 567 us (0.87)
  matrix products: 75.6 us -> 22.8 us
  loops' own time: 42.7 us -> 0 us
  Pallas kernels: 412 us -> 439 us
  local copies, waits for them, and re-layouts: 67.6 us -> 45 us
    dot_general x28 -> x0, matrix products: 54.9 us -> none  [the longest x4 15.7 us: attend_work(): jnp.einsum('gjqk,kgd->qgjd', probs.astype(jnp.bfloat16), values_part, pre...]
    another operation x18 -> x0, loops' own time: 42.7 us -> none  [the longest x1 21.2 us: sweep_keys(): carried, unused = lax.scan(sweep_step, carried, stacked)]
    pallas_call x11 -> x12, Pallas kernels: 412 us -> 439 us  [the longest x10 405 us: exchange(): pl.pallas_call(functools.partial(exchange_kernel, tuple((axis for axis, u...]
    reduce_sum x2, other arithmetic: 3.05 us -> 18.6 us  [norm_back(): jnp.mean(upstream * normed, axis=-1, keepdims=True)]
    dynamic_update_slice x8 -> x0, local copies, waits for them, and re-layouts: 10.7 us -> none  [attend_back(): lax.scan(grad_step, initial, stack_steps(all_keys, all_values, all_pos))]
    reduce_max x16 -> x0, other arithmetic: 10.3 us -> none  [outside(): jnp.max(key_pos) < jnp.min(query_start)]
    another operation x3 -> x1, local copies, waits for them, and re-layouts: 8.41 us -> 0.13 us  [local(): key_blocks = all_pos.reshape(-1, block_len)[:, 0] // block_len]
    while x11 -> x0, local copies, waits for them, and re-layouts: 6.59 us -> none  [the longest x2 5.58 us: sweep_keys(): carried, unused = lax.scan(sweep_step, carried, stacked)]
where the time goes in v2:
time: 567 us; the launch traced here: 559 us
  Pallas kernels  439 us (77%)
  other arithmetic  47.9 us (8%)
  local copies, waits for them, and re-layouts  45 us (8%)
  matrix products  22.8 us (4%)
    pallas_call x10, Pallas kernels, exchange(): pl.pallas_call(functools.partial(exchange_kernel, tuple((axis for axis, u...  405 us
    pallas_call x2, Pallas kernels, attention_call(): pl.pallas_call(functools.partial(kernel, *settings), out_shape=outputs, i...  34.4 us
    reduce_sum x2, other arithmetic, norm_back(): jnp.mean(upstream * normed, axis=-1, keepdims=True)  18.6 us

profile of v2, /device:TPU:9, one launch (start us, length us, event | category | flops | bytes accessed | tf_op | source)
XLA Modules:
  0.0 559.5 jit_solution(14742311152519348943)
XLA Ops:
  4.6 100.9 %shard_map.237 = (bf16[8,128,1024]{2,1,0:T(8,128)(2,1)S(1)}, bf16[4,128,1024]{2,1,0:T(8,128)(2,1)S(1)}, bf16[4,128,1024]{2,1,0:T(8,128)(2,1)S(1)}, bf16[8,128,51...) custom-call(bf16[128,1024]{1,0:T(8,128)(2,1)S(1)} %pad_maximum_fusio, ...), custom_call_target="tpu_custom_call" | custom-call | tf_op jit(solution)/shard_map/pallas_call | solution.py:261
  109.3 2.6 fusion.14
  118.4 68.0 %shard_map.238 = (bf16[8,512,256]{2,1,0:T(8,128)(2,1)S(1)}, bf16[8,512,256]{2,1,0:T(8,128)(2,1)S(1)}) custom-call(bf16[512,256]{1,0:T(8,128)(2,1)S(1)} %bitcast.117, bf16[512,256]{1,0:T(8,128)(2,1)S(1)} %slice.178.refs_1_), custom_call_target="tpu_custom_call" | custom-call | tf_op jit(solution)/shard_map/pallas_call | solution.py:261
  189.2 2.3 slice.123
  205.0 18.7 %shard_map.239 = (bf16[512,512]{1,0:T(8,128)(2,1)}, f32[4,512,1]{2,1,0:T(8,128)}) custom-call(s32[8]{0:T(128)} %and_select_fusion.blocks_ref, s32[1]{0:T(128)S(6)} %select_n.18.own_ref, bf16[512,512]{1,0:T(8,128)(2,1)} %convert_element_type.86.q_ref, bf16[4096,256]{1,0:T(8,128)(2,1)} %bitcast.102, bf16[4096,256]{1,0:T(8,128)(2,1)} %bitcast.104), custom_call_target="tpu_custom_call" | custom-call | tf_op jit(solution)/shard_map/pallas_call | solution.py:392
  225.6 10.9 %shard_map.240 = f32[128,1024]{1,0:T(8,128)S(1)} custom-call(bf16[4,128,1024]{2,1,0:T(8,128)(2,1)S(1)} %bitcast.114), custom_call_target="tpu_custom_call" | custom-call | tf_op jit(solution)/shard_map/pallas_call | solution.py:261
  236.8 9.9 %shard_map.241 = bf16[4,128,1024]{2,1,0:T(8,128)(2,1)S(1)} custom-call(bf16[128,1024]{1,0:T(8,128)(2,1)S(1)} %multiply_convert_fusion.4.refs_0_), custom_call_target="tpu_custom_call" | custom-call | tf_op jit(solution)/shard_map/pallas_call | solution.py:261
  250.0 3.6 convolution_convert_fusion
  256.4 15.5 %shard_map.242 = (f32[128,1024]{1,0:T(8,128)S(1)}, f32[128,1024]{1,0:T(8,128)S(1)}) custom-call(bf16[4,128,1024]{2,1,0:T(8,128)(2,1)S(1)} %bitcast.116, bf16[4,128,1024]{2,1,0:T(8,128)(2,1)S(1)} %bitcast.115), custom_call_target="tpu_custom_call" | custom-call | tf_op jit(solution)/shard_map/pallas_call | solution.py:261
  273.3 10.2 %shard_map.243 = bf16[4,128,1024]{2,1,0:T(8,128)(2,1)S(1)} custom-call(bf16[128,1024]{1,0:T(8,128)(2,1)S(1)} %get-tuple-element.113.refs_0_), custom_call_target="tpu_custom_call" | custom-call | tf_op jit(solution)/shard_map/pallas_call | solution.py:261
  292.9 15.7 %shard_map.244 = (f32[512,512]{1,0:T(8,128)}, bf16[4096,512]{1,0:T(8,128)(2,1)}) custom-call(s32[8]{0:T(128)} %and_select_fusion.blocks_ref, s32[1]{0:T(128)S(6)} %select_n.18.own_ref, bf16[512,512]{1,0:T(8,128)(2,1)} %convert_element_type.86.q_ref, bf16[4096,256]{1,0:T(8,128)(2,1)} %bitcast.103, bf16[4096,256]{1,0:T(8,128)(2,1)} %bitcast.105, ...), custom_call_target="tpu_custom_call" | custom-call | tf_op jit(solution)/shard_map/pallas_call | solution.py:392
  310.5 2.4 multiply_add_fusion
  312.9 16.5 %multiply_reduce_fusion.1 = (f32[512,2,2]{2,1,0:T(2,128)S(1)}, f32[512,2,2,128]{3,2,1,0:T(2,128)}) fusion(f32[512,2,2,128]{3,2,1,0:T(2,128)S(1)} %copy-done.15, f32[128]{0:T(128)S(1)} %copy-done.40, f32[512,2,2]{2,1,0:T(2,128)S(1)} %copy-done.22, f32[512,2,2,64]{3,2,1,0:T(2,128)S(1)} %get-tuple-element.125, f32[512,2,2,64]{3,2,1,0:T(2,128)S(1)} %get-tuple-element.124), kind=kLoop, calls=%fused_computation.18 | loop fusion | flops 1308672 | bytes 3162624 | tf_op jit(solution)/shard_map/reduce_sum | solution.py:59
  329.6 2.2 mul.451
  331.8 3.1 mul.452
  335.0 3.1 concatenate.39
  340.1 3.1 mul.433
  343.2 3.2 multiply_reduce_fusion
  346.5 73.0 %shard_map.245 = f32[512,512]{1,0:T(8,128)S(1)} custom-call(bf16[8,512,512]{2,1,0:T(8,128)(2,1)S(1)} %bitcast.106), custom_call_target="tpu_custom_call" | custom-call | tf_op jit(solution)/shard_map/pallas_call | solution.py:261
  429.8 2.6 convolution_convert_fusion.1
  433.8 10.2 %shard_map.246 = f32[128,1024]{1,0:T(8,128)S(1)} custom-call(bf16[4,128,1024]{2,1,0:T(8,128)(2,1)S(1)} %bitcast.113), custom_call_target="tpu_custom_call" | custom-call | tf_op jit(solution)/shard_map/pallas_call | solution.py:261
  444.3 4.9 shard_map.247
  449.2 2.2 convolution_convert_fusion.2
  451.3 101.7 %shard_map.248 = (f32[8,24,128]{2,1,0:T(8,128)S(1)}, f32[128,1024]{1,0:T(8,128)S(1)}, f32[128,1536]{1,0:T(8,128)S(1)}, f32[128,512]{1,0:T(8,128)S(1)}, f32[128,768]{1,0:T(8,128)S(1)}) custom-call(f32[24,128]{1,0:T(8,128)S(1)} %reduce_sum.166.refs_0_, bf16[8,128,1024]{2,1,0:T(8,128)(2,1)} %bitcast.138, bf16[8,128,1536]{2,1,0:T(8,128)(2,1)} %bitcast.135, ...), custom_call_target="tpu_custom_call" | custom-call | tf_op jit(solution)/shard_map/pallas_call | solution.py:261
  (166 shorter events, 68.9 us)
Async XLA Ops:
  0.6 3.5 copy-start.28
  0.7 3.6 copy-start.35
  0.7 3.6 copy-start.37
  0.7 3.6 copy-start.36
  0.7 3.6 copy-start.33
  0.7 3.8 copy-start.34
  0.7 3.9 copy-start.3
  113.2 3.3 copy-start.19
  115.7 81.4 %copy-start.24 = (f32[512,64]{1,0:T(8,128)}, f32[512,64]{1,0:T(8,128)S(1)}, u32[]{:S(2)}) copy-start(f32[512,64]{1,0:T(8,128)S(1)} %get-tuple-element.142) | copy-start | bytes 393220
  191.4 4.0 copy-start.40
  193.3 3.7 copy-start.14
  195.4 3.4 copy-start.21
  223.7 12.7 %copy-start.16 = (f32[128,1024]{1,0:T(8,128)S(1)}, f32[128,1024]{1,0:T(8,128)}, u32[]{:S(2)}) copy-start(f32[128,1024]{1,0:T(8,128)} %param.14) | copy-start | bytes 1572868
  225.6 11.1 %copy-start.38 = (f32[1024]{0:T(1024)S(1)}, f32[1024]{0:T(1024)}, u32[]{:S(2)}) copy-start(f32[1024]{0:T(1024)} %param.24) | copy-start | bytes 12292
  236.5 10.2 %copy-start.5 = (bf16[8,128,1536]{2,1,0:T(8,128)(2,1)S(1)}, bf16[8,128,1536]{2,1,0:T(8,128)(2,1)}, u32[]{:S(2)}) copy-start(bf16[8,128,1536]{2,1,0:T(8,128)(2,1)} %copy-done.4) | copy-start | bytes 9437188
  250.0 3.6 copy-start.42
  256.4 15.7 %copy-start.29 = (f32[128,1024]{1,0:T(8,128)S(1)}, f32[128,1024]{1,0:T(8,128)}, u32[]{:S(2)}) copy-start(f32[128,1024]{1,0:T(8,128)} %param.27) | copy-start | bytes 1572868
  272.1 11.5 %copy-start.31 = (bf16[512,512]{1,0:T(8,128)(2,1)S(1)}, bf16[512,512]{1,0:T(8,128)(2,1)}, u32[]{:S(2)}) copy-start(bf16[512,512]{1,0:T(8,128)(2,1)} %get-tuple-element.38) | copy-start | bytes 1572868
  331.8 6.2 %copy-start.23 = (f32[512,2,2]{2,1,0:T(2,128)S(1)}, f32[512,2,2]{2,1,0:T(2,128)}, u32[]{:S(2)}) copy-start(f32[512,2,2]{2,1,0:T(2,128)} %copy-done.21) | copy-start | bytes 24580
  343.2 3.2 copy-start.2
  432.4 11.5 %copy-start.17 = (f32[128,1024]{1,0:T(8,128)S(1)}, f32[128,1024]{1,0:T(8,128)}, u32[]{:S(2)}) copy-start(f32[128,1024]{1,0:T(8,128)} %param.14) | copy-start | bytes 1572868
  432.4 11.5 %copy-start.39 = (f32[1024]{0:T(1024)S(1)}, f32[1024]{0:T(1024)}, u32[]{:S(2)}) copy-start(f32[1024]{0:T(1024)} %param.23) | copy-start | bytes 12292
  553.0 5.3 copy-start.18
  553.0 5.3 copy-start.30
  (19 other events, 40.6 us)

commit v3 on v2

--- a/solution.py
+++ b/solution.py
@@ -27,16 +27,16 @@
     return (jnp.cos(angles), jnp.sin(angles))
 
 
-def spread_table(table, values):
-    half_width = values.shape[-1] // 2
-    table_shape = (table.shape[0],) + (1,) * (values.ndim - 2) + (half_width,)
-    return table.reshape(table_shape)
+def by_head(flat, width):
+    return jnp.stack([flat[:, at : at + width] for at in range(0, flat.shape[1], width)])
+
+
+def by_row(heads):
+    return jnp.concatenate([heads[head] for head in range(heads.shape[0])], axis=1)
 
 
 def rotate(values, cosine, sine_table):
     half_width = values.shape[-1] // 2
-    cosine = spread_table(cosine, values)
-    sine_table = spread_table(sine_table, values)
     former = values[..., :half_width]
     latter = values[..., half_width:]
     return jnp.concatenate(
@@ -46,8 +46,6 @@
 
 def rotate_back(grads, cosine, sine_table):
     half_width = grads.shape[-1] // 2
-    cosine = spread_table(cosine, grads)
-    sine_table = spread_table(sine_table, grads)
     former = grads[..., :half_width]
     latter = grads[..., half_width:]
     return jnp.concatenate(
@@ -419,7 +417,6 @@
     score_scale = head_width ** (-0.5)
     local_heads = q_weight.shape[1] // head_width
     local_groups = k_weight.shape[1] // head_width
-    group_size = local_heads // local_groups
     doc_len = positions.shape[0] * lax.axis_size("ctx") // DOCS
     qkv_shard = jnp.concatenate([q_weight, k_weight, v_weight], axis=1)
     pair_shard = jnp.concatenate([gate_weight, up_weight], axis=1)
@@ -447,10 +444,8 @@
     query_width = local_heads * head_width
     key_width = local_groups * head_width
     raw = jnp.dot(hidden_first, qkv_full, preferred_element_type=jnp.float32)
-    query_raw = raw[:, :query_width].reshape(block_len, local_groups, group_size, head_width)
-    key_raw = raw[:, query_width : query_width + key_width].reshape(
-        block_len, local_groups, head_width
-    )
+    query_raw = by_head(raw[:, :query_width], head_width)
+    key_raw = by_head(raw[:, query_width : query_width + key_width], head_width)
     values_local = raw[:, query_width + key_width :].astype(jnp.bfloat16)
     inv_query = inv_rms(query_raw)
     query_hat = query_raw * inv_query
@@ -458,9 +453,9 @@
     inv_key = inv_rms(key_raw)
     key_hat = key_raw * inv_key
     keys_local = rotate(key_hat * k_gain, cosine, sine_table).astype(jnp.bfloat16)
-    queries = queries.reshape(block_len, query_width)
+    queries = by_row(queries)
     all_keys, all_values = exchange(
-        [("ctx", keys_local.reshape(block_len, key_width)), ("ctx", values_local)], [], 2
+        [("ctx", by_row(keys_local)), ("ctx", values_local)], [], 2
     )
     settings = (score_scale, local_heads, local_groups, doc_len // block_len)
     attended_flat, log_total = attention_call(
@@ -536,26 +531,18 @@
         ],
         [],
     )
-    query_grad = query_grad.reshape(block_len, local_groups, group_size, head_width)
+    query_grad = by_head(query_grad, head_width)
     (stacked_grads,) = exchange([], [("ctx", key_terms)], 7)
-    stacked_grads = stacked_grads.reshape(block_len, 2, local_groups, head_width)
-    key_grad = stacked_grads[:, 0]
-    value_grad = stacked_grads[:, 1]
+    key_grad = by_head(stacked_grads[:, :key_width], head_width)
+    value_low = stacked_grads[:, key_width:].astype(jnp.bfloat16)
     query_back = rotate_back(query_grad, cosine, sine_table)
-    q_gain_part = jnp.sum(query_back * query_hat, axis=(0, 1, 2))
-    query_raw_grad = (
-        norm_back(query_back * q_gain, query_hat, inv_query)
-        .astype(jnp.bfloat16)
-        .reshape(block_len, query_width)
+    q_gain_part = jnp.sum(query_back * query_hat, axis=(0, 1))
+    query_raw_grad = by_row(
+        norm_back(query_back * q_gain, query_hat, inv_query).astype(jnp.bfloat16)
     )
     key_back = rotate_back(key_grad, cosine, sine_table)
     k_gain_part = jnp.sum(key_back * key_hat, axis=(0, 1))
-    key_raw_grad = (
-        norm_back(key_back * k_gain, key_hat, inv_key)
-        .astype(jnp.bfloat16)
-        .reshape(block_len, key_width)
-    )
-    value_low = value_grad.astype(jnp.bfloat16).reshape(block_len, key_width)
+    key_raw_grad = by_row(norm_back(key_back * k_gain, key_hat, inv_key).astype(jnp.bfloat16))
     qkv_grad = jnp.concatenate([query_raw_grad, key_raw_grad, value_low], axis=1)
     (hidden1_grad,) = exchange(
         [], [("tp", contract_last(qkv_grad, qkv_full).astype(jnp.bfloat16))], 8

time: 567 us -> 515 us (0.908); the launches traced: 559 us -> 518 us
  other arithmetic: 47.9 us -> 19.4 us
  local copies, waits for them, and re-layouts: 45 us -> 33.1 us
    reduce_sum x4 -> x1, other arithmetic: 21.8 us -> 0.91 us  [local(): q_gain_part = jnp.sum(query_back * query_hat, axis=(0, 1))]
    pallas_call x2, Pallas kernels: 34.4 us -> 18 us  [attention_call(): pl.pallas_call(functools.partial(kernel, *settings), out_shape=outputs, i...]
    pallas_call x10, Pallas kernels: 405 us -> 421 us  [exchange(): pl.pallas_call(functools.partial(exchange_kernel, tuple((axis for axis, u...]
    unnamed x92 -> x98, local copies, waits for them, and re-layouts: 8.78 us -> 21.2 us
    mul x8 -> x0, local copies, waits for them, and re-layouts: 11.7 us -> none  [the longest x3 5.91 us: norm_back(): normed * jnp.mean(upstream * normed, axis=-1, keepdims=True)]
    reshape x4 -> x0, local copies, waits for them, and re-layouts: 5.67 us -> none  [the longest x1 1.89 us: local(): raw[:, :query_width]]
where the time goes in v3:
time: 515 us; the launch traced here: 518 us
  Pallas kernels  439 us (85%)
  local copies, waits for them, and re-layouts  33.1 us (6%)
  matrix products  22.2 us (4%)
  other arithmetic  19.4 us (4%)
    pallas_call x10, Pallas kernels, exchange(): pl.pallas_call(functools.partial(exchange_kernel, tuple((axis for axis, u...  421 us
    unnamed x98, local copies, waits for them, and re-layouts  21.2 us
    pallas_call x2, Pallas kernels, attention_call(): pl.pallas_call(functools.partial(kernel, *settings), out_shape=outputs, i...  18 us

profile of v3, /device:TPU:9, one launch (start us, length us, event | category | flops | bytes accessed | tf_op | source)
XLA Modules:
  0.0 517.7 jit_solution(14391177861464214040)
XLA Ops:
  11.8 100.9 %shard_map.237 = (bf16[8,128,1024]{2,1,0:T(8,128)(2,1)S(1)}, bf16[4,128,1024]{2,1,0:T(8,128)(2,1)S(1)}, bf16[4,128,1024]{2,1,0:T(8,128)(2,1)S(1)}, bf16[8,128,51...) custom-call(bf16[128,1024]{1,0:T(8,128)(2,1)S(1)} %pad_maximum_fusio, ...), custom_call_target="tpu_custom_call" | custom-call | tf_op jit(solution)/shard_map/pallas_call | solution.py:259
  119.5 3.2 fusion.26
  126.2 68.0 %shard_map.238 = (bf16[8,512,256]{2,1,0:T(8,128)(2,1)S(1)}, bf16[8,512,256]{2,1,0:T(8,128)(2,1)S(1)}) custom-call(bf16[512,256]{1,0:T(8,128)(2,1)S(1)} %pad_maximum_fusion.12.refs_0_, bf16[512,256]{1,0:T(8,128)(2,1)S(1)} %slice.354.refs_1_), custom_call_target="tpu_custom_call" | custom-call | tf_op jit(solution)/shard_map/pallas_call | solution.py:259
  196.9 9.0 %shard_map.239 = (bf16[512,512]{1,0:T(8,128)(2,1)}, f32[4,512,1]{2,1,0:T(8,128)}) custom-call(s32[8]{0:T(128)} %and_select_fusion.blocks_ref, s32[1]{0:T(128)S(6)} %select_n.18.own_ref, bf16[512,512]{1,0:T(8,128)(2,1)} %pad_maximum_fusion.7.q_ref, bf16[4096,256]{1,0:T(8,128)(2,1)} %bitcast.122, bf16[4096,256]{1,0:T(8,128)(2,1)} %bitcast.124), custom_call_target="tpu_custom_call" | custom-call | tf_op jit(solution)/shard_map/pallas_call | solution.py:390
  208.1 1.8 convolution_convert_fusion.7
  209.9 10.9 %shard_map.240 = f32[128,1024]{1,0:T(8,128)S(1)} custom-call(bf16[4,128,1024]{2,1,0:T(8,128)(2,1)S(1)} %bitcast.134), custom_call_target="tpu_custom_call" | custom-call | tf_op jit(solution)/shard_map/pallas_call | solution.py:259
  221.1 10.0 %shard_map.241 = bf16[4,128,1024]{2,1,0:T(8,128)(2,1)S(1)} custom-call(bf16[128,1024]{1,0:T(8,128)(2,1)S(1)} %multiply_convert_fusion.5.refs_0_), custom_call_target="tpu_custom_call" | custom-call | tf_op jit(solution)/shard_map/pallas_call | solution.py:259
  231.2 1.8 fusion.27
  235.5 1.8 convolution_convert_fusion.5
  237.4 15.4 %shard_map.242 = (f32[128,1024]{1,0:T(8,128)S(1)}, f32[128,1024]{1,0:T(8,128)S(1)}) custom-call(bf16[4,128,1024]{2,1,0:T(8,128)(2,1)S(1)} %bitcast.136, bf16[4,128,1024]{2,1,0:T(8,128)(2,1)S(1)} %bitcast.135), custom_call_target="tpu_custom_call" | custom-call | tf_op jit(solution)/shard_map/pallas_call | solution.py:259
  254.3 3.5 convolution_convert_fusion
  258.9 9.9 %shard_map.243 = bf16[4,128,1024]{2,1,0:T(8,128)(2,1)S(1)} custom-call(bf16[128,1024]{1,0:T(8,128)(2,1)S(1)} %get-tuple-element.100.refs_0_), custom_call_target="tpu_custom_call" | custom-call | tf_op jit(solution)/shard_map/pallas_call | solution.py:259
  268.7 1.9 convert_multiply_fusion
  271.4 2.5 reshape.232
  273.9 2.6 reduce_sum.140
  278.1 9.0 %shard_map.244 = (f32[512,512]{1,0:T(8,128)}, bf16[4096,512]{1,0:T(8,128)(2,1)}) custom-call(s32[8]{0:T(128)} %and_select_fusion.blocks_ref, s32[1]{0:T(128)S(6)} %select_n.18.own_ref, bf16[512,512]{1,0:T(8,128)(2,1)} %pad_maximum_fusion.7.q_ref, bf16[4096,256]{1,0:T(8,128)(2,1)} %bitcast.123, bf16[4096,256]{1,0:T(8,128)(2,1)} %bitcast.125, ...), custom_call_target="tpu_custom_call" | custom-call | tf_op jit(solution)/shard_map/pallas_call | solution.py:390
  287.1 2.2 copy-done.2
  289.3 89.3 %shard_map.245 = f32[512,512]{1,0:T(8,128)S(1)} custom-call(bf16[8,512,512]{2,1,0:T(8,128)(2,1)S(1)} %bitcast.126), custom_call_target="tpu_custom_call" | custom-call | tf_op jit(solution)/shard_map/pallas_call | solution.py:259
  386.0 2.7 convolution_convert_fusion.1
  388.7 10.2 %shard_map.246 = f32[128,1024]{1,0:T(8,128)S(1)} custom-call(bf16[4,128,1024]{2,1,0:T(8,128)(2,1)S(1)} %bitcast.133), custom_call_target="tpu_custom_call" | custom-call | tf_op jit(solution)/shard_map/pallas_call | solution.py:259
  400.1 4.8 shard_map.247
  405.0 101.4 %shard_map.248 = (f32[8,24,128]{2,1,0:T(8,128)S(1)}, f32[128,1024]{1,0:T(8,128)S(1)}, f32[128,1536]{1,0:T(8,128)S(1)}, f32[128,512]{1,0:T(8,128)S(1)}, f32[128,768]{1,0:T(8,128)S(1)}) custom-call(f32[24,128]{1,0:T(8,128)S(1)} %reduce_sum.148.refs_0_, bf16[8,128,1024]{2,1,0:T(8,128)(2,1)} %bitcast.155, bf16[8,128,1536]{2,1,0:T(8,128)(2,1)} %bitcast.154, ...), custom_call_target="tpu_custom_call" | custom-call | tf_op jit(solution)/shard_map/pallas_call | solution.py:259
  508.6 1.8 copy.46
  514.9 1.9 copy.47
  (159 shorter events, 47.2 us)
Async XLA Ops:
  0.6 10.0 %copy-start.32 = (f32[128,1024]{1,0:T(8,128)S(1)}, f32[128,1024]{1,0:T(8,128)}, u32[]{:S(2)}) copy-start(f32[128,1024]{1,0:T(8,128)} %param.27) | copy-start | bytes 1572868
  0.7 10.1 %copy-start.37 = (bf16[128,768]{1,0:T(8,128)(2,1)S(1)}, bf16[128,768]{1,0:T(8,128)(2,1)}, u32[]{:S(2)}) copy-start(bf16[128,768]{1,0:T(8,128)(2,1)} %param.21) | copy-start | bytes 589828
  0.7 10.1 %copy-start.38 = (bf16[128,768]{1,0:T(8,128)(2,1)S(1)}, bf16[128,768]{1,0:T(8,128)(2,1)}, u32[]{:S(2)}) copy-start(bf16[128,768]{1,0:T(8,128)(2,1)} %param.20) | copy-start | bytes 589828
  0.7 9.1 %copy-start.39 = (bf16[128,512]{1,0:T(8,128)(2,1)S(1)}, bf16[128,512]{1,0:T(8,128)(2,1)}, u32[]{:S(2)}) copy-start(bf16[128,512]{1,0:T(8,128)(2,1)} %param.16) | copy-start | bytes 393220
  5.7 6.0 %copy-start.6 = (s32[512]{0:T(512)S(1)}, s32[512]{0:T(512)}, u32[]{:S(2)}) copy-start(s32[512]{0:T(512)} %param.15) | copy-start | bytes 6148
  11.8 112.8 %copy-start.18 = (f32[512,64]{1,0:T(8,128)}, f32[512,64]{1,0:T(8,128)S(1)}, u32[]{:S(2)}) copy-start(f32[512,64]{1,0:T(8,128)S(1)} %get-tuple-element.143) | copy-start | bytes 393220
  112.7 1.6 copy-start.7
  114.3 1.4 copy-start.9
  122.9 1.4 copy-start.20
  122.9 1.4 copy-start.22
  122.9 1.4 copy-start.24
  195.5 1.4 copy-start.1
  208.1 12.7 %copy-start.17 = (f32[128,1024]{1,0:T(8,128)S(1)}, f32[128,1024]{1,0:T(8,128)}, u32[]{:S(2)}) copy-start(f32[128,1024]{1,0:T(8,128)} %param.14) | copy-start | bytes 1572868
  209.9 11.1 %copy-start.40 = (f32[1024]{0:T(1024)S(1)}, f32[1024]{0:T(1024)}, u32[]{:S(2)}) copy-start(f32[1024]{0:T(1024)} %param.24) | copy-start | bytes 12292
  220.8 10.3 %copy-start.8 = (bf16[8,128,1536]{2,1,0:T(8,128)(2,1)S(1)}, bf16[8,128,1536]{2,1,0:T(8,128)(2,1)}, u32[]{:S(2)}) copy-start(bf16[8,128,1536]{2,1,0:T(8,128)(2,1)} %copy-done.7) | copy-start | bytes 9437188
  231.2 1.8 copy-start.12
  231.2 1.8 copy-start.16
  237.4 15.7 %copy-start.33 = (f32[128,1024]{1,0:T(8,128)S(1)}, f32[128,1024]{1,0:T(8,128)}, u32[]{:S(2)}) copy-start(f32[128,1024]{1,0:T(8,128)} %param.27) | copy-start | bytes 1572868
  257.8 10.9 %copy-start.36 = (bf16[512,512]{1,0:T(8,128)(2,1)S(1)}, bf16[512,512]{1,0:T(8,128)(2,1)}, u32[]{:S(2)}) copy-start(bf16[512,512]{1,0:T(8,128)(2,1)} %get-tuple-element.38) | copy-start | bytes 1572868
  287.1 2.2 copy-start.2
  289.3 89.3 %copy-start.35 = (f32[512,512]{1,0:T(8,128)S(1)}, f32[512,512]{1,0:T(8,128)}, u32[]{:S(2)}) copy-start(f32[512,512]{1,0:T(8,128)} %get-tuple-element.46) | copy-start | bytes 3145732
  383.1 1.6 copy-start.10
  386.0 12.8 %copy-start.41 = (f32[1024]{0:T(1024)S(1)}, f32[1024]{0:T(1024)}, u32[]{:S(2)}) copy-start(f32[1024]{0:T(1024)} %param.23) | copy-start | bytes 12292
  388.7 10.4 %copy-start.34 = (f32[128,1024]{1,0:T(8,128)S(1)}, f32[128,1024]{1,0:T(8,128)}, u32[]{:S(2)}) copy-start(f32[128,1024]{1,0:T(8,128)} %get-tuple-element.101) | copy-start | bytes 1572868
  (20 other events, 20.7 us)
